TPU v7x, 128 devices: a whole 4x4x4 slice. The times are simulated.
128 devices in a mesh: row: 16 (over z_lo, y, core), col: 8 (over x, z_hi).
Axes of the slice: x: 4, y: 4, z: 4 (z_hi: 2, z_lo: 2; z = z_hi * 2 + z_lo), core: 2. Of those that a mesh axis runs over, the one named last changes fastest.
Arguments:
- hamiltonian: bfloat16 [8192, 8192], P('row', 'col'), may hold values from -1 to 1, as said below
- block_cols: int32 [128, 26], P('row'), may hold values from 0 to 127, as said below
- start_vectors: bfloat16 [8192, 2048], P('col'), may hold values from -6 to 6
Outputs:
- filtered: bfloat16 [8192, 2048], P('col')
- correlation: float32 [2048, 2048], P('row', 'col')
- projected: float32 [2048, 2048], P('row', 'col')
Inputs may be any that keep to these rules, and one draw needn't show every extreme that they name: `block_cols`: along the last dimension, 26 distinct block columns in increasing order; block row i lists itself, and lists j exactly when block row j lists i. `hamiltonian`: Symmetric.
All inputs are finite; a program needn't handle non-finite values.
Results may differ from a plain program's by a relative error of at most 0.02.
Values may be sent and summed in bfloat16 or wider, within the bound.
A program may use at most 128 MiB of HBM per device.

v0:
```python
import jax
import jax.numpy as jnp
from jax import lax
from jax.sharding import PartitionSpec as P

BLK = 64


center_point = 0.2
half_width = 0.8


def spread(x, axis, root):
    mine = lax.axis_index(axis) == root
    return lax.psum(jnp.where(mine, x, jnp.zeros_like(x)), axis)


def shards(hamiltonian, block_cols, start_vectors):
    row_index = lax.axis_index("row")
    col_index = lax.axis_index("col")
    row_span = hamiltonian.shape[0]
    col_span = hamiltonian.shape[1]
    band_count = row_span // BLK
    col_blocks = col_span // BLK
    targets = col_index * col_blocks + jnp.arange(col_blocks, dtype=jnp.int32)
    block_mask = jnp.any(block_cols[:, :, None] == targets[None, None, :], axis=1)
    tile_blocks = hamiltonian.reshape(band_count, BLK, col_blocks, BLK)
    masked_tile = jnp.where(
        block_mask[:, None, :, None], tile_blocks, jnp.zeros_like(tile_blocks)
    ).reshape(row_span, col_span)
    offset = row_index * row_span - col_index * col_span
    active = (offset >= 0) & (offset < col_span)
    clamped = jnp.clip(offset, 0, col_span - row_span)
    diagonal_weight = jnp.where(active, -center_point, 0.0).astype(jnp.float32)
    own_start = lax.dynamic_slice_in_dim(start_vectors, clamped, row_span, 0).astype(jnp.float32)
    first_term = (
        jnp.dot(masked_tile, start_vectors, preferred_element_type=jnp.float32)
        + diagonal_weight * own_start
    )
    section_one = (lax.psum(first_term, "col") / half_width).astype(jnp.bfloat16)
    second_term = lax.dot_general(
        masked_tile, section_one, (((0,), (0,)), ((), ())), preferred_element_type=jnp.float32
    )
    diagonal_rows = lax.dynamic_slice_in_dim(
        second_term, clamped, row_span, 0
    ) + diagonal_weight * section_one.astype(jnp.float32)
    second_term = lax.dynamic_update_slice_in_dim(second_term, diagonal_rows, clamped, 0)
    summed = lax.psum(second_term, "row")
    filtered = (2.0 / half_width * summed - start_vectors.astype(jnp.float32)).astype(jnp.bfloat16)
    mirror_root = row_index * row_span // col_span
    held_rows = lax.dynamic_slice_in_dim(filtered, clamped, row_span, 0)
    row_filtered = spread(held_rows, "col", mirror_root)
    image_term = jnp.dot(masked_tile, filtered, preferred_element_type=jnp.float32)
    image = lax.psum(image_term.astype(jnp.bfloat16), "col")
    vector_cols = filtered.shape[1]
    col_piece = vector_cols // lax.axis_size("col")
    right_side = jnp.concatenate(
        (
            lax.dynamic_slice_in_dim(row_filtered, col_index * col_piece, col_piece, 1),
            lax.dynamic_slice_in_dim(image, col_index * col_piece, col_piece, 1),
        ),
        axis=1,
    )
    projections = lax.psum_scatter(
        lax.dot_general(
            row_filtered, right_side, (((0,), (0,)), ((), ())), preferred_element_type=jnp.float32
        ).astype(jnp.bfloat16),
        "row",
        scatter_dimension=0,
        tiled=True,
    ).astype(jnp.float32)
    order_total = col_span * lax.axis_size("col")
    correlation = projections[:, :col_piece] / order_total
    projected = projections[:, col_piece:] / order_total
    return (filtered, correlation, projected)


def solution(mesh):
    in_specs = (P("row", "col"), P("row", None), P("col", None))
    out_specs = (P("col", None), P("row", "col"), P("row", "col"))
    return jax.shard_map(shards, mesh=mesh, in_specs=in_specs, out_specs=out_specs, check_vma=False)
```

profile of v0, /device:TPU:1, one launch (start us, length us, event | category | flops | bytes accessed | tf_op | source)
XLA Modules:
  0.0 649.7 jit_solution(8817459942375690126)
XLA Ops:
  7.2 0.0 all-reduce.5.cloned.1.call-start
  7.2 1.0 compare_reduce_fusion
  8.2 0.3 broadcast_in_dim.19
  8.6 2.4 broadcast_in_dim.20
  10.9 7.6 %multiply_add_fusion.1 = f32[512,2048]{1,0:T(8,128)} fusion(bf16[1024,2048]{1,0:T(8,128)(2,1)} %param.5, s32[]{:T(128)S(6)} %min.4, f32[]{:T(128)S(6)} %select_n.31, pred[512,1024]{1,0:T(32,128)(4,1)S(1)} %broadcast_in_dim.20, bf16[512,1024]{1,0:T(8,128)(2,1)} %param.3), kind=kOutput, calls=%fused_computation.3 | convolution fusion | flops 2151153664 | bytes 12058632 | tf_op jit(solution)/shard_map/dot_general | solution.py:37
  18.5 0.0 all-reduce.5.cloned.1.call-update
  18.6 0.0 all-reduce.7.cloned.1.call-start
  18.6 189.0 %all-reduce.5.cloned.1.call-done = f32[512,2048]{1,0:T(8,128)} async-done(((f32[512,2048]{1,0:T(8,128)}), f32[512,2048]{1,0:T(8,128)}) %all-reduce.5.cloned.1.call-update) | async-done | bytes 4194320 | tf_op jit(solution)/shard_map/psum | solution.py:40
  207.6 0.0 copy-done.3
  207.6 4.8 fusion
  212.4 0.0 copy-start
  212.4 3.2 copy-done
  215.6 0.0 copy-done.1
  215.6 2.9 multiply_add_fusion
  218.5 11.3 %dynamic_update_slice.3 = f32[1024,2048]{1,0:T(8,128)} dynamic-update-slice(f32[1024,2048]{1,0:T(8,128)} %copy-done, f32[512,2048]{1,0:T(8,128)} %multiply_add_fusion, s32[]{:T(128)S(6)} %min.4, s32[]{:T(128)} %constant.42.clone.1) | dynamic-update-slice | bytes 8388612 | tf_op jit(solution)/shard_map/dynamic_update_slice | solution.py:47
  229.9 0.0 all-reduce.7.cloned.1.call-update
  229.9 0.0 all-reduce.9.cloned.1.call-start
  230.0 144.2 %all-reduce.7.cloned.1.call-done = f32[1024,2048]{1,0:T(8,128)} async-done(((f32[1024,2048]{1,0:T(8,128)}), f32[1024,2048]{1,0:T(8,128)}) %all-reduce.7.cloned.1.call-update) | async-done | bytes 8388624 | tf_op jit(solution)/shard_map/psum | solution.py:48
  374.2 6.1 subtract_convert_fusion
  380.3 0.0 copy-start.2
  380.4 3.7 convolution_convert_fusion
  384.1 0.0 copy-done.2
  384.1 1.9 dynamic-slice_select_fusion
  386.0 0.0 all-reduce.9.cloned.1.call-update
  386.0 0.0 reduce-scatter.2.cloned.1.call-start
  386.1 188.1 %all-reduce.9.cloned.1.call-done = (bf16[512,2048]{1,0:T(8,128)(2,1)}, bf16[512,2048]{1,0:T(8,128)(2,1)}) async-done(((bf16[512,2048]{1,0:T(8,128)(2,1)}, bf16[512,2048]{1,0:T(8,128)(2,1)}), (bf16[512,2048]{1,0:T(8,128)(2,1)}, bf16[512,2048]{1,0:T(8,128)(2,1)})) %all-reduce.9.cloned.1.call-update) | async-done | bytes 4194320 | tf_op jit(solution)/shard_map/psum | solution.py:15
  574.2 1.1 constant_dynamic-slice_fusion
  575.3 4.2 convolution_convert_fusion.1
  579.5 0.0 reduce-scatter.2.cloned.1.call-update
  579.5 62.0 %reduce-scatter.2.cloned.1.call-done = bf16[128,512]{1,0:T(8,128)(2,1)} async-done(((bf16[2048,512]{1,0:T(8,128)(2,1)}), bf16[128,512]{1,0:T(8,128)(2,1)}) %reduce-scatter.2.cloned.1.call-update) | async-done | bytes 131088 | tf_op jit(solution)/shard_map/reduce_scatter | solution.py:64
  641.5 0.9 convert_element_type.31
  642.4 0.7 slice_multiply_fusion
  (3 shorter events, 0.0 us)
Async XLA Ops:
  7.2 200.4 %all-reduce.5.cloned.1.call-start = ((), (), s32[]{:S(2)}) async-start(), calls=%async_computation.1 | async-start | bytes 8388608 | tf_op jit(solution)/shard_map/psum | solution.py:40
  18.5 189.1 %copy-start.3 = (bf16[512,1024]{1,0:T(8,128)(2,1)S(1)}, bf16[512,1024]{1,0:T(8,128)(2,1)}, u32[]{:S(2)}) copy-start(bf16[512,1024]{1,0:T(8,128)(2,1)} %param.3) | copy-start | bytes 3145732
  18.6 355.7 %all-reduce.7.cloned.1.call-start = ((), (), s32[]{:S(2)}) async-start(), calls=%async_computation.2 | async-start | bytes 16777216 | tf_op jit(solution)/shard_map/psum | solution.py:48
  207.6 8.0 %copy-start.1 = (f32[512,2048]{1,0:T(8,128)S(1)}, f32[512,2048]{1,0:T(8,128)}, u32[]{:S(2)}) copy-start(f32[512,2048]{1,0:T(8,128)} %all-reduce.5.cloned.1.call-done) | copy-start | bytes 12582916
  212.4 3.2 copy-start
  229.9 344.3 %all-reduce.9.cloned.1.call-start = ((), (), s32[]{:S(2)}) async-start(), calls=%async_computation.4 | async-start | bytes 8388608 | tf_op jit(solution)/shard_map/psum | solution.py:15
  380.3 3.7 copy-start.2
  386.0 255.5 %reduce-scatter.2.cloned.1.call-start = ((), (), s32[]{:S(2)}) async-start(), calls=%async_computation.3 | async-start | bytes 2228224 | tf_op jit(solution)/shard_map/reduce_scatter | solution.py:64
Sparse Core Ops, SparseCore 0:
  18.7 188.8 all-reduce.4
  230.0 144.1 all-reduce.6
  386.1 188.0 all-reduce.8
  579.6 61.8 reduce-scatter.1
where the time goes:
time: 653 us; the launch traced here: 650 us
  waiting for transfers between devices  583 us (89%)
  matrix products  20.2 us (3%)
  local copies, waits for them, and re-layouts  18.3 us (3%)
  between operations  13.9 us (2%)
  other arithmetic  13.6 us (2%)
    psum x1, waiting for transfers between devices, shards(): lax.psum(first_term, 'col') / half_width  189 us
    psum x1, waiting for transfers between devices, spread(): return lax.psum(jnp.where(mine, x, jnp.zeros_like(x)), axis)  188 us
    psum x1, waiting for transfers between devices, shards(): summed = lax.psum(second_term, 'row')  144 us
    reduce_scatter x1, waiting for transfers between devices, shards(): lax.psum_scatter(lax.dot_general(row_filtered, right_side, (((0,), (0,)),...  62 us
  transfers between devices with their start and end apart: 4, of which 4 were waited for; matrix products, arithmetic and copies ran while one was open for 0% of the time, Pallas kernels for 0%

commit v1 on v0

v1 whole, which is shorter than its diff:
```python
import functools

import jax
import jax.numpy as jnp
from jax import lax
from jax.experimental import pallas as pl
from jax.experimental.pallas import tpu as pltpu
from jax.sharding import PartitionSpec as P

BLK = 64
K_NB = 26
DEPTH = K_NB * BLK
MESH = pl.DeviceIdType.MESH
center_point = 0.2
half_width = 0.8


class Gather:
    def __init__(self, slot, p, w, pair, right, left, send_sem, recv_sem, pending):
        self.slot, self.p, self.w = slot, p, w
        self.pair, self.right, self.left = pair, right, left
        self.send_sem, self.recv_sem, self.pending = send_sem, recv_sem, pending

    def at(self, dp, dw):
        return lax.rem(self.p + dp + 4, 4), (self.w + dw) % 2

    def sent(self, i):
        return self.at(*((0, 0), (0, 0), (0, 0), (0, 1), (0, 1), (-1, 0), (1, 1))[i])

    def received(self, i):
        return self.at(*((0, 1), (-1, 0), (1, 0), (-1, 1), (1, 1), (2, 0), (2, 1))[i])

    def send(self, i, chunk=0, src=None):
        dst = self.slot(*self.sent(i), chunk)
        to = self.pair if i == 0 else (self.right if i % 2 else self.left)
        copy = pltpu.make_async_remote_copy(
            src_ref=dst if src is None else src,
            dst_ref=dst,
            send_sem=self.send_sem.at[i, chunk],
            recv_sem=self.recv_sem.at[i, chunk],
            device_id=to,
            device_id_type=MESH,
        )
        copy.start()
        self.pending.append(copy)

    def wait(self, i, chunk=0):
        ref = self.slot(*self.received(i), chunk)
        pltpu.make_async_remote_copy(
            src_ref=ref,
            dst_ref=ref,
            send_sem=self.send_sem.at[i, chunk],
            recv_sem=self.recv_sem.at[i, chunk],
            device_id=self.pair,
            device_id_type=MESH,
        ).wait_recv()


def kernel(
    h_ref, lists_ref, x_ref, f_ref, corr_ref, proj_ref,
    panels, lists, sib_list, index, halves, sib_half, packed, xs, ss, fs, rows, image, stack,
    turned, part, parts,
    own_sem, panel_sems, list_sems, sib_list_sem, index_sem, half_sem, h_sems, h_sib_sems,
    x_sems, s_sems, f_sems, r_sems, r_sib_sems, part_sems, out_sem,
):
    r = lax.axis_index("row")
    c = lax.axis_index("col")
    k = lax.rem(r, 2)
    chip = r // 2
    y = lax.rem(chip, 4)
    zl = r // 8
    x = c // 2
    zh = lax.rem(c, 2)
    sibling = (r + 1 - 2 * k, c)
    pending = []

    def ring(v, d):
        return lax.rem(v + d + 4, 4)

    def row_device(z, yy):
        return (z * 8 + yy * 2 + k, c)

    def col_device(xx, z):
        return (r, xx * 2 + z)

    def remote(src, dst, sems, i, to, start=True):
        copy = pltpu.make_async_remote_copy(
            src_ref=src, dst_ref=dst, send_sem=sems.at[0, i], recv_sem=sems.at[1, i],
            device_id=to, device_id_type=MESH,
        )
        if start:
            copy.start()
            pending.append(copy)
        return copy

    row_peers = [((zl + dz) % 2, ring(y, dy)) for dz in (1, 0) for dy in (0, 1, 3, 2) if dz or dy]
    col_peers = [(ring(x, dx), (zh + dw) % 2) for dw in (1, 0) for dx in (2, 1, 3, 0) if dw or dx]

    own_panel = pltpu.make_async_copy(
        h_ref.at[:, :, pl.ds(pl.multiple_of((2 * y + zl) * 128, 128), 128)],
        panels.at[pl.ds(chip * 8, 8)], own_sem.at[0],
    )
    own_panel.start()
    x_src = x_ref.at[:, :, pl.ds(pl.multiple_of(r * 128, 128), 128)]
    own_x = pltpu.make_async_copy(x_src, xs.at[pl.ds(c * 16, 16)], own_sem.at[1])
    own_x.start()
    lists[chip] = jnp.zeros((8, 128), jnp.int32)
    lists[chip, :, :K_NB] = lists_ref[...]
    panels[64] = jnp.zeros((BLK, 128), jnp.bfloat16)

    barrier = pltpu.get_barrier_semaphore()
    for z, yy in row_peers:
        pl.semaphore_signal(barrier, inc=1, device_id=row_device(z, yy), device_id_type=MESH)
    for xx, z in col_peers:
        pl.semaphore_signal(barrier, inc=1, device_id=col_device(xx, z), device_id_type=MESH)
    pl.semaphore_signal(barrier, inc=1, device_id=sibling, device_id_type=MESH)
    pl.semaphore_wait(barrier, 15)

    list_copies, panel_copies = [], []
    for i, (z, yy) in enumerate(row_peers):
        list_copies.append(remote(lists.at[chip], lists.at[chip], list_sems, i, row_device(z, yy)))
    for i, (z, yy) in enumerate(row_peers):
        src = h_ref.at[:, :, pl.ds(pl.multiple_of((2 * yy + z) * 128, 128), 128)]
        panel_copies.append(remote(src, panels.at[pl.ds(chip * 8, 8)], panel_sems, i, row_device(z, yy)))

    def col_gather(buffer, sems, size, order):
        def slot(p, w, t):
            return buffer.at[pl.ds((p * 2 + w) * 16 + order[t] * size, size)]

        return Gather(slot, x, zh, col_device(x, 1 - zh), col_device(ring(x, 1), zh), col_device(ring(x, -1), zh),
                      sems.at[0], sems.at[1], pending)

    gx = col_gather(xs, x_sems, 16, (0,))
    for i in range(3):
        gx.send(i, 0, x_src)

    for copy in list_copies:
        copy.wait_recv()
    sib_lists = remote(lists.at[c], sib_list, sib_list_sem, 0, sibling)
    mine = pltpu.make_async_copy(lists.at[c], index.at[pl.ds(k * 8, 8)], index_sem.at[0])
    mine.start()
    sib_lists.wait_recv()
    theirs = pltpu.make_async_copy(sib_list, index.at[pl.ds((1 - k) * 8, 8)], index_sem.at[1])
    theirs.start()
    mine.wait()
    theirs.wait()

    own_x.wait()
    gx.wait(0)
    gx.send(3)
    gx.send(4)
    gx.wait(1)
    gx.send(5)

    own_panel.wait()
    for copy in panel_copies:
        copy.wait_recv()
    pair_column = 4 * y + 2 * zl
    lane = lax.broadcasted_iota(jnp.int32, (BLK, 128), 1)
    line = lax.broadcasted_iota(jnp.int32, (BLK, 128), 0)
    for side in range(2):
        for s in range(K_NB):
            i = index[pair_column + side, s]
            local = jnp.where(lax.rem(i // 8, 2) == k, 8 * (i // 16) + lax.rem(i, 8), 64)
            stack[s * BLK:(s + 1) * BLK, :] = panels[local]
        pick = (lane == line + BLK * side).astype(jnp.bfloat16)
        halves[side] = lax.dot_general(
            pick, stack[...], (((1,), (1,)), ((), ())), preferred_element_type=jnp.float32
        ).astype(jnp.bfloat16)
    swap = remote(halves.at[1 - k], sib_half, half_sem, 0, sibling)
    swap.wait_recv()
    packed[pair_column + k] = halves[k] + sib_half[...]

    def h_slot(p, w, t):
        return packed.at[p * 4 + w * 2 + k]

    def row_gather(slot, sems):
        return Gather(slot, y, zl, row_device(1 - zl, y), row_device(zl, ring(y, 1)), row_device(zl, ring(y, -1)),
                      sems.at[0], sems.at[1], pending)

    gh = row_gather(h_slot, h_sems)
    h_sib = {}

    def pass_h(i):
        slot = h_slot(y, zl, 0) if i == 0 else h_slot(*gh.received(i - 1), 0)
        h_sib[i] = remote(slot, slot, h_sib_sems, i, sibling)

    for i in range(3):
        gh.send(i)
    pass_h(0)

    gx.wait(2)
    gx.wait(3)
    gx.wait(4)
    gx.send(6)

    def product(source, column):
        for s in range(K_NB):
            stack[s * BLK:(s + 1) * BLK, :] = source[index[column, s]]
        return jnp.dot(packed[column], stack[...], preferred_element_type=jnp.float32)

    order = (y, ring(y, -1), ring(y, 1), ring(y, 2))
    gs = col_gather(ss, s_sems, 4, order)

    def first_degree(t):
        @pl.loop(0, 4)
        def _(j):
            column = order[t] * 4 + j
            at = c * 16 + column
            total = product(xs, column) - center_point * xs[at].astype(jnp.float32)
            ss[at] = (total / half_width).astype(jnp.bfloat16)

        for i in range(3):
            gs.send(i, t)

    def early(g, t):
        g.wait(0, t)
        g.send(3, t)
        g.send(4, t)
        g.wait(1, t)
        g.send(5, t)

    def late(g, t):
        g.wait(4, t)
        g.send(6, t)

    def rest(g, t):
        for i in (2, 3, 5, 6):
            g.wait(i, t)

    gh.wait(0)
    gh.send(3)
    gh.send(4)
    pass_h(1)
    gx.wait(5)
    gx.wait(6)
    h_sib[0].wait_recv()
    h_sib[1].wait_recv()
    first_degree(0)
    gh.wait(1)
    gh.send(5)
    pass_h(2)
    gh.wait(2)
    pass_h(3)
    gh.wait(4)
    gh.send(6)
    pass_h(5)
    gh.wait(3)
    pass_h(4)
    early(gs, 0)
    h_sib[2].wait_recv()
    h_sib[4].wait_recv()
    first_degree(1)
    h_sib[3].wait_recv()
    h_sib[5].wait_recv()
    first_degree(2)
    late(gs, 0)
    early(gs, 1)
    gh.wait(5)
    pass_h(6)
    gh.wait(6)
    pass_h(7)
    early(gs, 2)
    h_sib[6].wait_recv()
    h_sib[7].wait_recv()
    first_degree(3)
    late(gs, 1)
    late(gs, 2)
    early(gs, 3)
    late(gs, 3)
    for t in range(4):
        rest(gs, t)

    gf = col_gather(fs, f_sems, 4, (0, 1, 2, 3))

    def r_slot(parity):
        def slot(p, w, t):
            return rows.at[w * 8 + p * 2 + parity, pl.ds(4 * t, 4)]

        return slot

    gr = row_gather(r_slot(k), r_sems)
    r_sib = {}

    def pass_r(i, t):
        place = (y, zl) if i == 0 else gr.received(i - 1)
        slot = r_slot(k)(*place, t)
        r_sib[i, t] = remote(slot, slot, r_sib_sems, i * 4 + t, sibling)

    for t in range(4):
        @pl.loop(0, 4)
        def _(j):
            column = t * 4 + j
            at = c * 16 + column
            total = product(ss, column) - center_point * ss[at].astype(jnp.float32)
            out = ((2.0 / half_width) * total - xs[at].astype(jnp.float32)).astype(jnp.bfloat16)
            fs[at] = out
            rows[r, column] = out

        for i in range(3):
            gf.send(i, t)
            gr.send(i, t)
        pass_r(0, t)

    for t in range(4):
        early(gf, t)
        early(gr, t)
        pass_r(1, t)
        pass_r(2, t)
        gr.wait(2, t)
        pass_r(3, t)
    for t in range(4):
        late(gf, t)
        late(gr, t)
        pass_r(5, t)
        gr.wait(3, t)
        pass_r(4, t)
    outs = []

    def write_out(group, i):
        copy = pltpu.make_async_copy(
            rows.at[group], f_ref.at[:, :, pl.ds(pl.multiple_of(group * 128, 128), 128)], out_sem.at[i]
        )
        copy.start()
        outs.append(copy)

    for t in range(4):
        gr.wait(5, t)
        pass_r(6, t)
        gr.wait(6, t)
        pass_r(7, t)
    places = [(y, zl)] + [gr.received(i) for i in range(7)]
    for i, (p, w) in enumerate(places):
        write_out(w * 8 + p * 2 + k, i)
    for t in range(4):
        for i in range(8):
            r_sib[i, t].wait_recv()
    for i, (p, w) in enumerate(places):
        write_out(w * 8 + p * 2 + 1 - k, 8 + i)
    for t in range(4):
        rest(gf, t)

    unit = (lax.broadcasted_iota(jnp.int32, (128, 128), 0) == lax.broadcasted_iota(jnp.int32, (128, 128), 1))
    unit = unit.astype(jnp.bfloat16)

    def turn(block):
        turned[...] = lax.dot_general(
            unit, block.reshape(1024, 128), (((1,), (1,)), ((), ())), preferred_element_type=jnp.float32
        ).astype(jnp.bfloat16)

    def project(which):
        def to(place, group):
            def column(half):
                block = rows[group * 2 + half].reshape(1024, 128)
                return jnp.dot(turned[...], block, preferred_element_type=jnp.float32).astype(jnp.bfloat16)

            for half in range(2):
                place[:, half * 128:(half + 1) * 128] = column(half)

        copies = []
        for i, (xx, z) in enumerate(col_peers):
            group = xx * 2 + z
            to(part.at[which, group], group)
            copies.append(
                remote(part.at[which, group], parts.at[which, c], part_sems, which * 7 + i, col_device(xx, z))
            )
        to(parts.at[which, c], c)
        return copies

    turn(fs[pl.ds(c * 16, 16)])
    corr_copies = project(0)

    @pl.loop(0, 16)
    def _(column):
        image[column] = product(fs, column).astype(jnp.bfloat16)

    turn(image[...])
    proj_copies = project(1)

    for copy in corr_copies:
        copy.wait_recv()
    corr_ref[...] = jnp.sum(parts[0].astype(jnp.float32), axis=0) / 8192.0
    for copy in proj_copies:
        copy.wait_recv()
    proj_ref[...] = jnp.sum(parts[1].astype(jnp.float32), axis=0) / 8192.0
    for copy in outs:
        copy.wait()
    for copy in pending:
        copy.wait_send()


def shards(hamiltonian, block_cols, start_vectors):
    bf16, f32, dma = jnp.bfloat16, jnp.float32, pltpu.SemaphoreType.DMA
    vmem = pltpu.VMEM
    f, corr, proj = pl.pallas_call(
        kernel,
        out_shape=(
            jax.ShapeDtypeStruct((16, BLK, 2048), bf16),
            jax.ShapeDtypeStruct((128, 256), f32),
            jax.ShapeDtypeStruct((128, 256), f32),
        ),
        in_specs=[
            pl.BlockSpec(memory_space=pl.ANY),
            pl.BlockSpec(memory_space=pltpu.VMEM),
            pl.BlockSpec(memory_space=pl.ANY),
        ],
        out_specs=(
            pl.BlockSpec(memory_space=pl.ANY),
            pl.BlockSpec(memory_space=pltpu.VMEM),
            pl.BlockSpec(memory_space=pltpu.VMEM),
        ),
        scratch_shapes=[
            vmem((65, BLK, 128), bf16),
            vmem((8, 8, 128), jnp.int32),
            vmem((8, 128), jnp.int32),
            pltpu.SMEM((16, 128), jnp.int32),
            vmem((2, BLK, DEPTH), bf16),
            vmem((BLK, DEPTH), bf16),
            vmem((16, BLK, DEPTH), bf16),
            vmem((128, BLK, 128), bf16),
            vmem((128, BLK, 128), bf16),
            vmem((128, BLK, 128), bf16),
            vmem((16, 16, BLK, 128), bf16),
            vmem((16, BLK, 128), bf16),
            vmem((DEPTH, 128), bf16),
            vmem((128, 1024), bf16),
            vmem((2, 8, 128, 256), bf16),
            vmem((2, 8, 128, 256), bf16),
            dma((2,)),
            dma((2, 7)),
            dma((2, 7)),
            dma((2, 1)),
            dma((2,)),
            dma((2, 1)),
            dma((2, 7, 1)),
            dma((2, 8)),
            dma((2, 7, 1)),
            dma((2, 7, 4)),
            dma((2, 7, 4)),
            dma((2, 7, 4)),
            dma((2, 32)),
            dma((2, 14)),
            dma((16,)),
        ],
        compiler_params=pltpu.CompilerParams(
            collective_id=0, has_side_effects=True, vmem_limit_bytes=48 * 1024 * 1024
        ),
    )(hamiltonian.reshape(8, BLK, 1024), block_cols, start_vectors.reshape(16, BLK, 2048))
    return f.reshape(1024, 2048), corr, proj


def solution(mesh):
    in_specs = (P("row", "col"), P("row", None), P("col", None))
    out_specs = (P("col", None), P("row", "col"), P("row", "col"))
    return jax.shard_map(shards, mesh=mesh, in_specs=in_specs, out_specs=out_specs, check_vma=False)
```

time: 653 us -> 115 us (0.18)
  waiting for transfers between devices: 583 us -> 0 us
  Pallas kernels: 0 us -> 109 us
  matrix products: 20.2 us -> 0 us
  other arithmetic: 13.6 us -> 0 us
  between operations: 13.9 us -> 0.65 us
  local copies, waits for them, and re-layouts: 18.3 us -> 5.23 us
    psum x3 -> x0, waiting for transfers between devices: 521 us -> none  [the longest x1 189 us: shards(): lax.psum(first_term, 'col') / half_width]
    pallas_call x0 -> x1, Pallas kernels: none -> 109 us  [shards(): pl.pallas_call(kernel, out_shape=(jax.ShapeDtypeStruct((16, BLK, 2048), b...]
    reduce_scatter x1 -> x0, waiting for transfers between devices: 62 us -> none  [shards(): lax.psum_scatter(lax.dot_general(row_filtered, right_side, (((0,), (0,)),...]
    dot_general x4 -> x0, matrix products: 20.2 us -> none  [the longest x1 7.58 us: shards(): jnp.dot(masked_tile, start_vectors, preferred_element_type=jnp.float32)]
    dynamic_update_slice x1 -> x0, local copies, waits for them, and re-layouts: 11.3 us -> none  [shards(): lax.dynamic_update_slice_in_dim(second_term, diagonal_rows, clamped, 0)]
    convert_element_type x2 -> x0, other arithmetic: 7.06 us -> none  [the longest x1 6.14 us: shards(): (2.0 / half_width * summed - start_vectors.astype(jnp.float32)).astype(jn...]
  transfers between devices with their start and end apart: 4 -> 0, of which waited for: 4 -> 0; matrix products, arithmetic and copies ran while one was open for 0% -> 0% of each run, Pallas kernels for 0% -> 0%
where the time goes in v1:
time: 115 us
  Pallas kernels  109 us (95%)
  local copies, waits for them, and re-layouts  5.23 us (5%)
    pallas_call x1, Pallas kernels, shards(): pl.pallas_call(kernel, out_shape=(jax.ShapeDtypeStruct((16, BLK, 2048), b...  109 us
    unnamed x7, local copies, waits for them, and re-layouts  5.23 us

profile of v1, /device:TPU:1, one launch (start us, length us, event | category | flops | bytes accessed | tf_op | source)
XLA Modules:
  0.0 114.9 jit_solution(3970980621622831314)
XLA Ops:
  0.6 0.0 copy-start
  0.6 1.2 %copy-done = bf16[512,1024]{1,0:T(8,128)(2,1)S(1)} copy-done((bf16[512,1024]{1,0:T(8,128)(2,1)S(1)}, bf16[512,1024]{1,0:T(8,128)(2,1)}, u32[]{:S(2)}) %copy-start) | copy-done | bytes 1048600
  1.9 0.0 copy-start.1
  1.9 0.7 copy-done.1
  2.5 109.0 %shard_map.58 = (bf16[16,64,2048]{2,1,0:T(8,128)(2,1)S(1)}, f32[128,256]{1,0:T(8,128)S(1)}, f32[128,256]{1,0:T(8,128)S(1)}) custom-call(bf16[8,64,1024]{2,1,0:T(8,128)(2,1)S(1)} %bitcast.4, s32[8,26]{1,0:T(8,128)S(1)} %copy-done.1, bf16[16,64,2048]{2,1,0:T(8,128)(2,1)} %bitcast.5), custom_call_target="tpu_custom_call" | custom-call | tf_op jit(solution)/shard_map/pallas_call | solution.py:395
  111.6 2.0 %copy.9 = bf16[1024,2048]{1,0:T(8,128)(2,1)} copy(bf16[1024,2048]{1,0:T(8,128)(2,1)S(1)} %bitcast.3) | data formatting | bytes 8388608
  113.6 0.7 copy.10
  114.2 0.7 copy.11
Async XLA Ops:
  0.6 1.2 %copy-start = (bf16[512,1024]{1,0:T(8,128)(2,1)S(1)}, bf16[512,1024]{1,0:T(8,128)(2,1)}, u32[]{:S(2)}) copy-start(bf16[512,1024]{1,0:T(8,128)(2,1)} %param.3) | copy-start | bytes 3145732
  1.9 0.7 copy-start.1

commit v2 on v1

--- a/solution.py
+++ b/solution.py
@@ -1,5 +1,3 @@
-import functools
-
 import jax
 import jax.numpy as jnp
 from jax import lax
@@ -59,7 +57,7 @@
 def kernel(
     h_ref, lists_ref, x_ref, f_ref, corr_ref, proj_ref,
     panels, lists, sib_list, index, halves, sib_half, packed, xs, ss, fs, rows, image, stack,
-    turned, part, parts,
+    own_lists, part, parts,
     own_sem, panel_sems, list_sems, sib_list_sem, index_sem, half_sem, h_sems, h_sib_sems,
     x_sems, s_sems, f_sems, r_sems, r_sib_sems, part_sems, out_sem,
 ):
@@ -104,8 +102,11 @@
     x_src = x_ref.at[:, :, pl.ds(pl.multiple_of(r * 128, 128), 128)]
     own_x = pltpu.make_async_copy(x_src, xs.at[pl.ds(c * 16, 16)], own_sem.at[1])
     own_x.start()
+    read_lists = pltpu.make_async_copy(lists_ref, own_lists, own_sem.at[2])
+    read_lists.start()
+    read_lists.wait()
     lists[chip] = jnp.zeros((8, 128), jnp.int32)
-    lists[chip, :, :K_NB] = lists_ref[...]
+    lists[chip, :, :K_NB] = own_lists[...]
     panels[64] = jnp.zeros((BLK, 128), jnp.bfloat16)
 
     barrier = pltpu.get_barrier_semaphore()
@@ -113,8 +114,10 @@
         pl.semaphore_signal(barrier, inc=1, device_id=row_device(z, yy), device_id_type=MESH)
     for xx, z in col_peers:
         pl.semaphore_signal(barrier, inc=1, device_id=col_device(xx, z), device_id_type=MESH)
-    pl.semaphore_signal(barrier, inc=1, device_id=sibling, device_id_type=MESH)
-    pl.semaphore_wait(barrier, 15)
+    across = (lax.rem(r + 8, 16), x * 2 + 1 - zh)
+    for device in (sibling, across):
+        pl.semaphore_signal(barrier, inc=1, device_id=device, device_id_type=MESH)
+    pl.semaphore_wait(barrier, 16)
 
     list_copies, panel_copies = [], []
     for i, (z, yy) in enumerate(row_peers):
@@ -123,16 +126,18 @@
         src = h_ref.at[:, :, pl.ds(pl.multiple_of((2 * yy + z) * 128, 128), 128)]
         panel_copies.append(remote(src, panels.at[pl.ds(chip * 8, 8)], panel_sems, i, row_device(z, yy)))
 
-    def col_gather(buffer, sems, size, order):
+    def col_gather(buffer, sems, size, starts, pair):
         def slot(p, w, t):
-            return buffer.at[pl.ds((p * 2 + w) * 16 + order[t] * size, size)]
-
-        return Gather(slot, x, zh, col_device(x, 1 - zh), col_device(ring(x, 1), zh), col_device(ring(x, -1), zh),
+            return buffer.at[pl.ds((p * 2 + w) * 16 + starts[t], size)]
+
+        return Gather(slot, x, zh, pair, col_device(ring(x, 1), zh), col_device(ring(x, -1), zh),
                       sems.at[0], sems.at[1], pending)
 
-    gx = col_gather(xs, x_sems, 16, (0,))
-    for i in range(3):
-        gx.send(i, 0, x_src)
+    gx = col_gather(xs, x_sems, 16, (0,), across)
+    x_across = x_ref.at[:, :, pl.ds(pl.multiple_of(lax.rem(r + 8, 16) * 128, 128), 128)]
+    gx.send(0, 0, x_across)
+    gx.send(1, 0, x_src)
+    gx.send(2, 0, x_src)
 
     for copy in list_copies:
         copy.wait_recv()
@@ -189,36 +194,36 @@
         gh.send(i)
     pass_h(0)
 
-    gx.wait(2)
-    gx.wait(3)
     gx.wait(4)
     gx.send(6)
+    for i in (2, 3, 5, 6):
+        gx.wait(i)
 
     def product(source, column):
-        for s in range(K_NB):
-            stack[s * BLK:(s + 1) * BLK, :] = source[index[column, s]]
-        return jnp.dot(packed[column], stack[...], preferred_element_type=jnp.float32)
-
-    order = (y, ring(y, -1), ring(y, 1), ring(y, 2))
-    gs = col_gather(ss, s_sems, 4, order)
-
-    def first_degree(t):
-        @pl.loop(0, 4)
-        def _(j):
-            column = order[t] * 4 + j
+        stacked = jnp.concatenate([source[index[column, s]] for s in range(K_NB)], axis=0)
+        return jnp.dot(packed[column], stacked, preferred_element_type=jnp.float32)
+
+    pairs = [gh.at(*d) for d in ((0, 0), (0, 1), (-1, 0), (1, 0), (1, 1), (-1, 1), (2, 0), (2, 1))]
+    starts = [4 * p + 2 * w for p, w in pairs]
+    across_z = col_device(x, 1 - zh)
+    gs = col_gather(ss, s_sems, 2, starts, across_z)
+
+    def first_degree(t, sib):
+        h_sib[sib].wait_recv()
+        for j in range(2):
+            column = starts[t] + j
             at = c * 16 + column
             total = product(xs, column) - center_point * xs[at].astype(jnp.float32)
             ss[at] = (total / half_width).astype(jnp.bfloat16)
-
         for i in range(3):
             gs.send(i, t)
 
     def early(g, t):
+        g.wait(1, t)
+        g.send(5, t)
         g.wait(0, t)
         g.send(3, t)
         g.send(4, t)
-        g.wait(1, t)
-        g.send(5, t)
 
     def late(g, t):
         g.wait(4, t)
@@ -228,50 +233,52 @@
         for i in (2, 3, 5, 6):
             g.wait(i, t)
 
+    first_degree(0, 0)
     gh.wait(0)
     gh.send(3)
     gh.send(4)
     pass_h(1)
-    gx.wait(5)
-    gx.wait(6)
-    h_sib[0].wait_recv()
-    h_sib[1].wait_recv()
-    first_degree(0)
     gh.wait(1)
     gh.send(5)
     pass_h(2)
     gh.wait(2)
     pass_h(3)
+    first_degree(1, 1)
+    first_degree(2, 2)
+    first_degree(3, 3)
+    early(gs, 0)
     gh.wait(4)
     gh.send(6)
     pass_h(5)
+    early(gs, 1)
     gh.wait(3)
     pass_h(4)
-    early(gs, 0)
-    h_sib[2].wait_recv()
-    h_sib[4].wait_recv()
-    first_degree(1)
-    h_sib[3].wait_recv()
-    h_sib[5].wait_recv()
-    first_degree(2)
+    early(gs, 2)
+    early(gs, 3)
+    first_degree(4, 5)
+    first_degree(5, 4)
     late(gs, 0)
-    early(gs, 1)
+    late(gs, 1)
     gh.wait(5)
     pass_h(6)
+    early(gs, 4)
+    early(gs, 5)
+    first_degree(6, 6)
     gh.wait(6)
     pass_h(7)
-    early(gs, 2)
-    h_sib[6].wait_recv()
-    h_sib[7].wait_recv()
-    first_degree(3)
-    late(gs, 1)
     late(gs, 2)
-    early(gs, 3)
     late(gs, 3)
-    for t in range(4):
+    early(gs, 6)
+    first_degree(7, 7)
+    late(gs, 4)
+    late(gs, 5)
+    late(gs, 6)
+    early(gs, 7)
+    late(gs, 7)
+    for t in range(8):
         rest(gs, t)
 
-    gf = col_gather(fs, f_sems, 4, (0, 1, 2, 3))
+    gf = col_gather(fs, f_sems, 4, (0, 4, 8, 12), across_z)
 
     def r_slot(parity):
         def slot(p, w, t):
@@ -282,80 +289,70 @@
     gr = row_gather(r_slot(k), r_sems)
     r_sib = {}
 
-    def pass_r(i, t):
-        place = (y, zl) if i == 0 else gr.received(i - 1)
-        slot = r_slot(k)(*place, t)
-        r_sib[i, t] = remote(slot, slot, r_sib_sems, i * 4 + t, sibling)
-
-    for t in range(4):
-        @pl.loop(0, 4)
-        def _(j):
+    def pass_r(i):
+        p, w = (y, zl) if i == 0 else gr.received(i - 1)
+        slot = rows.at[w * 8 + p * 2 + k]
+        r_sib[i] = remote(slot, slot, r_sib_sems, i, sibling)
+
+    outs = []
+
+    def write_out(group, i):
+        copy = pltpu.make_async_copy(
+            rows.at[group], f_ref.at[:, :, pl.ds(pl.multiple_of(group * 128, 128), 128)], out_sem.at[i]
+        )
+        copy.start()
+        outs.append(copy)
+
+    for t in range(4):
+        for j in range(4):
             column = t * 4 + j
             at = c * 16 + column
             total = product(ss, column) - center_point * ss[at].astype(jnp.float32)
             out = ((2.0 / half_width) * total - xs[at].astype(jnp.float32)).astype(jnp.bfloat16)
             fs[at] = out
             rows[r, column] = out
-
-        for i in range(3):
+        for i in (1, 2, 0):
             gf.send(i, t)
             gr.send(i, t)
-        pass_r(0, t)
-
-    for t in range(4):
+    pass_r(0)
+    for t in range(4):
+        early(gr, t)
         early(gf, t)
-        early(gr, t)
-        pass_r(1, t)
-        pass_r(2, t)
+    pass_r(1)
+    pass_r(2)
+    for t in range(4):
         gr.wait(2, t)
-        pass_r(3, t)
-    for t in range(4):
+    pass_r(3)
+    for t in range(4):
+        late(gr, t)
         late(gf, t)
-        late(gr, t)
-        pass_r(5, t)
+    pass_r(5)
+    for t in range(4):
         gr.wait(3, t)
-        pass_r(4, t)
-    outs = []
-
-    def write_out(group, i):
-        copy = pltpu.make_async_copy(
-            rows.at[group], f_ref.at[:, :, pl.ds(pl.multiple_of(group * 128, 128), 128)], out_sem.at[i]
-        )
-        copy.start()
-        outs.append(copy)
-
+    pass_r(4)
+    places = [(y, zl)] + [gr.received(i) for i in range(7)]
+    for i, (p, w) in enumerate(places[:6]):
+        write_out(w * 8 + p * 2 + k, i)
     for t in range(4):
         gr.wait(5, t)
-        pass_r(6, t)
+    pass_r(6)
+    for t in range(4):
         gr.wait(6, t)
-        pass_r(7, t)
-    places = [(y, zl)] + [gr.received(i) for i in range(7)]
+    pass_r(7)
+    for i in (6, 7):
+        p, w = places[i]
+        write_out(w * 8 + p * 2 + k, i)
     for i, (p, w) in enumerate(places):
-        write_out(w * 8 + p * 2 + k, i)
-    for t in range(4):
-        for i in range(8):
-            r_sib[i, t].wait_recv()
-    for i, (p, w) in enumerate(places):
+        r_sib[i].wait_recv()
         write_out(w * 8 + p * 2 + 1 - k, 8 + i)
-    for t in range(4):
-        rest(gf, t)
-
-    unit = (lax.broadcasted_iota(jnp.int32, (128, 128), 0) == lax.broadcasted_iota(jnp.int32, (128, 128), 1))
-    unit = unit.astype(jnp.bfloat16)
-
-    def turn(block):
-        turned[...] = lax.dot_general(
-            unit, block.reshape(1024, 128), (((1,), (1,)), ((), ())), preferred_element_type=jnp.float32
-        ).astype(jnp.bfloat16)
-
-    def project(which):
+
+    def project(which, left):
         def to(place, group):
-            def column(half):
-                block = rows[group * 2 + half].reshape(1024, 128)
-                return jnp.dot(turned[...], block, preferred_element_type=jnp.float32).astype(jnp.bfloat16)
-
             for half in range(2):
-                place[:, half * 128:(half + 1) * 128] = column(half)
+                place[:, half * 128:(half + 1) * 128] = lax.dot_general(
+                    left, rows[group * 2 + half].reshape(1024, 128), (((0,), (0,)), ((), ())),
+                    preferred_element_type=jnp.float32,
+                ).astype(jnp.bfloat16)
 
         copies = []
         for i, (xx, z) in enumerate(col_peers):
@@ -367,15 +364,17 @@
         to(parts.at[which, c], c)
         return copies
 
-    turn(fs[pl.ds(c * 16, 16)])
-    corr_copies = project(0)
-
-    @pl.loop(0, 16)
-    def _(column):
-        image[column] = product(fs, column).astype(jnp.bfloat16)
-
-    turn(image[...])
-    proj_copies = project(1)
+    corr_copies = project(0, fs[pl.ds(c * 16, 16)].reshape(1024, 128))
+    for t in range(4):
+        rest(gf, t)
+
+    @pl.loop(0, 4)
+    def _(j):
+        for i in range(4):
+            column = j * 4 + i
+            image[column] = product(fs, column).astype(jnp.bfloat16)
+
+    proj_copies = project(1, image[...].reshape(1024, 128))
 
     for copy in corr_copies:
         copy.wait_recv()
@@ -392,23 +391,17 @@
 def shards(hamiltonian, block_cols, start_vectors):
     bf16, f32, dma = jnp.bfloat16, jnp.float32, pltpu.SemaphoreType.DMA
     vmem = pltpu.VMEM
-    f, corr, proj = pl.pallas_call(
+    place = pl.BlockSpec(memory_space=pl.ANY)
+    out_shape = (
+        jax.ShapeDtypeStruct((16, BLK, 2048), bf16),
+        jax.ShapeDtypeStruct((128, 256), f32),
+        jax.ShapeDtypeStruct((128, 256), f32),
+    )
+    results = pl.pallas_call(
         kernel,
-        out_shape=(
-            jax.ShapeDtypeStruct((16, BLK, 2048), bf16),
-            jax.ShapeDtypeStruct((128, 256), f32),
-            jax.ShapeDtypeStruct((128, 256), f32),
-        ),
-        in_specs=[
-            pl.BlockSpec(memory_space=pl.ANY),
-            pl.BlockSpec(memory_space=pltpu.VMEM),
-            pl.BlockSpec(memory_space=pl.ANY),
-        ],
-        out_specs=(
-            pl.BlockSpec(memory_space=pl.ANY),
-            pl.BlockSpec(memory_space=pltpu.VMEM),
-            pl.BlockSpec(memory_space=pltpu.VMEM),
-        ),
+        out_shape=out_shape,
+        in_specs=[place] * 3,
+        out_specs=(place, pl.BlockSpec(memory_space=pltpu.VMEM), pl.BlockSpec(memory_space=pltpu.VMEM)),
         scratch_shapes=[
             vmem((65, BLK, 128), bf16),
             vmem((8, 8, 128), jnp.int32),
@@ -423,10 +416,10 @@
             vmem((16, 16, BLK, 128), bf16),
             vmem((16, BLK, 128), bf16),
             vmem((DEPTH, 128), bf16),
-            vmem((128, 1024), bf16),
+            vmem((8, K_NB), jnp.int32),
             vmem((2, 8, 128, 256), bf16),
             vmem((2, 8, 128, 256), bf16),
-            dma((2,)),
+            dma((3,)),
             dma((2, 7)),
             dma((2, 7)),
             dma((2, 1)),
@@ -435,17 +428,36 @@
             dma((2, 7, 1)),
             dma((2, 8)),
             dma((2, 7, 1)),
+            dma((2, 7, 8)),
             dma((2, 7, 4)),
             dma((2, 7, 4)),
-            dma((2, 7, 4)),
-            dma((2, 32)),
+            dma((2, 8)),
             dma((2, 14)),
             dma((16,)),
         ],
         compiler_params=pltpu.CompilerParams(
-            collective_id=0, has_side_effects=True, vmem_limit_bytes=48 * 1024 * 1024
+            collective_id=0, has_side_effects=True, vmem_limit_bytes=62 * 1024 * 1024
         ),
     )(hamiltonian.reshape(8, BLK, 1024), block_cols, start_vectors.reshape(16, BLK, 2048))
+
+    def hand_on(*refs):
+        sources, targets, sems = refs[:3], refs[3:6], refs[6]
+        copies = [pltpu.make_async_copy(a.at[4 * i:4 * i + 4], b.at[4 * i:4 * i + 4], sems.at[i])
+                  for a, b in (refs[0:4:3],) for i in range(4)]
+        copies += [pltpu.make_async_copy(sources[i], targets[i], sems.at[3 + i]) for i in (1, 2)]
+        for copy in copies:
+            copy.start()
+        for copy in copies:
+            copy.wait()
+
+    f, corr, proj = pl.pallas_call(
+        hand_on,
+        out_shape=out_shape,
+        in_specs=[place] * 3,
+        out_specs=(place,) * 3,
+        scratch_shapes=[dma((6,))],
+        compiler_params=pltpu.CompilerParams(vmem_limit_bytes=62 * 1024 * 1024),
+    )(*results)
     return f.reshape(1024, 2048), corr, proj
 
 

time: 115 us -> 239 us (2.08)
  Pallas kernels: 109 us -> 238 us
  local copies, waits for them, and re-layouts: 5.23 us -> 0 us
    pallas_call x1 -> x2, Pallas kernels: 109 us -> 238 us  [the longest x1 136 us: shards(): pl.pallas_call(hand_on, out_shape=out_shape, in_specs=[place] * 3, out_sp...]
    unnamed x7 -> x0, local copies, waits for them, and re-layouts: 5.23 us -> none
where the time goes in v2:
time: 239 us
  Pallas kernels  238 us (100%)
    pallas_call x1, Pallas kernels, shards(): pl.pallas_call(hand_on, out_shape=out_shape, in_specs=[place] * 3, out_sp...  136 us
    pallas_call x1, Pallas kernels, shards(): pl.pallas_call(kernel, out_shape=out_shape, in_specs=[place] * 3, out_spe...  102 us

profile of v2, /device:TPU:1, one launch (start us, length us, event | category | flops | bytes accessed | tf_op | source)
XLA Modules:
  0.0 238.6 jit_solution(4833552342017706815)
XLA Ops:
  0.6 101.8 %shard_map.58 = (bf16[16,64,2048]{2,1,0:T(8,128)(2,1)}, f32[128,256]{1,0:T(8,128)}, f32[128,256]{1,0:T(8,128)}) custom-call(bf16[8,64,1024]{2,1,0:T(8,128)(2,1)} %bitcast.4, s32[8,26]{1,0:T(8,128)} %lists_ref.1, bf16[16,64,2048]{2,1,0:T(8,128)(2,1)} %bitcast.3), custom_call_target="tpu_custom_call" | custom-call | tf_op jit(solution)/shard_map/pallas_call | solution.py:400
  102.5 136.2 %shard_map.59 = (bf16[16,64,2048]{2,1,0:T(8,128)(2,1)}, f32[128,256]{1,0:T(8,128)}, f32[128,256]{1,0:T(8,128)}) custom-call(bf16[16,64,2048]{2,1,0:T(8,128)(2,1)} %get-tuple-element.9.refs_0_, f32[128,256]{1,0:T(8,128)} %get-tuple-element.10.refs_1_, f32[128,256]{1,0:T(8,128)} %get-tuple-element.11.refs_2_), custom_call_target="tpu_custom_call" | custom-call | tf_op jit(solution)/shard_map/pallas_call | solution.py:453

commit v3 on v2

--- a/solution.py
+++ b/solution.py
@@ -12,12 +12,33 @@
 center_point = 0.2
 half_width = 0.8
 
+FIRST = (
+    ("x", 5, 0), ("x", 3, 0), ("x", 4, 0), ("x", 5, 1), ("x", 3, 1), ("x", 4, 1), ("pack",), ("swap",), ("x", 6, 0),
+    ("add",), ("h", 0, 0), ("h", 1, 0), ("h", 2, 0), ("p", 0, 0), ("h", 0, 1), ("h", 1, 1), ("h", 2, 1), ("p", 0, 1),
+    ("x", 6, 1), ("h", 3, 0), ("h", 4, 0), ("p", 1, 0), ("h", 5, 0), ("p", 2, 0), ("p", 3, 0), ("h", 3, 1),
+    ("h", 4, 1), ("p", 1, 1), ("h", 5, 1), ("p", 2, 1), ("p", 3, 1), ("s", 0), ("g", 5, 0), ("s", 1), ("g", 3, 0),
+    ("g", 4, 0), ("p", 4, 0), ("h", 6, 0), ("p", 5, 0), ("s", 2), ("s", 3), ("p", 6, 0), ("h", 6, 1), ("p", 5, 1),
+    ("g", 5, 1), ("g", 3, 1), ("g", 4, 1), ("g", 6, 0), ("g", 5, 2), ("s", 4), ("g", 3, 2), ("g", 4, 2), ("p", 4, 1),
+    ("p", 7, 0), ("g", 5, 3), ("g", 3, 3), ("g", 4, 3), ("g", 6, 1), ("s", 5), ("g", 6, 2), ("p", 6, 1), ("p", 7, 1),
+    ("g", 3, 4), ("g", 4, 4), ("g", 5, 4), ("s", 6), ("g", 6, 3), ("s", 7), ("g", 3, 5), ("g", 4, 5), ("g", 5, 5),
+    ("g", 6, 4), ("g", 3, 6), ("g", 4, 6), ("g", 5, 6), ("g", 3, 7), ("g", 4, 7), ("g", 5, 7), ("g", 6, 5),
+    ("g", 6, 6), ("g", 6, 7),
+)
+SECOND = (
+    ("f", 0), ("f", 1), ("f", 2), ("f", 3), ("q", 0), ("r", 5, 0), ("r", 3, 0), ("r", 4, 0), ("a", 5, 0), ("a", 3, 0),
+    ("a", 4, 0), ("r", 5, 1), ("r", 3, 1), ("r", 4, 1), ("a", 5, 1), ("a", 3, 1), ("a", 4, 1), ("r", 5, 2),
+    ("r", 3, 2), ("r", 4, 2), ("a", 5, 2), ("a", 3, 2), ("a", 4, 2), ("r", 5, 3), ("r", 3, 3), ("r", 4, 3),
+    ("a", 5, 3), ("a", 3, 3), ("a", 4, 3), ("q", 1), ("q", 2), ("q", 3), ("r", 6, 0), ("a", 6, 0), ("r", 6, 1),
+    ("a", 6, 1), ("r", 6, 2), ("a", 6, 2), ("r", 6, 3), ("a", 6, 3), ("q", 5), ("q", 4), ("q", 6), ("q", 7),
+)
+
 
 class Gather:
     def __init__(self, slot, p, w, pair, right, left, send_sem, recv_sem, pending):
         self.slot, self.p, self.w = slot, p, w
         self.pair, self.right, self.left = pair, right, left
         self.send_sem, self.recv_sem, self.pending = send_sem, recv_sem, pending
+        self.waited = set()
 
     def at(self, dp, dw):
         return lax.rem(self.p + dp + 4, 4), (self.w + dw) % 2
@@ -42,7 +63,10 @@
         copy.start()
         self.pending.append(copy)
 
-    def wait(self, i, chunk=0):
+    def need(self, i, chunk=0):
+        if (i, chunk) in self.waited:
+            return
+        self.waited.add((i, chunk))
         ref = self.slot(*self.received(i), chunk)
         pltpu.make_async_remote_copy(
             src_ref=ref,
@@ -53,10 +77,15 @@
             device_id_type=MESH,
         ).wait_recv()
 
+    def step(self, i, chunk=0):
+        if i >= 3:
+            self.need((0, 0, 1, 4)[i - 3], chunk)
+        self.send(i, chunk)
+
 
 def kernel(
     h_ref, lists_ref, x_ref, f_ref, corr_ref, proj_ref,
-    panels, lists, sib_list, index, halves, sib_half, packed, xs, ss, fs, rows, image, stack,
+    panels, lists, sib_list, index, halves, sib_half, packed, xs, ss, fs, rows, image,
     own_lists, part, parts,
     own_sem, panel_sems, list_sems, sib_list_sem, index_sem, half_sem, h_sems, h_sib_sems,
     x_sems, s_sems, f_sems, r_sems, r_sib_sems, part_sems, out_sem,
@@ -122,22 +151,22 @@
     list_copies, panel_copies = [], []
     for i, (z, yy) in enumerate(row_peers):
         list_copies.append(remote(lists.at[chip], lists.at[chip], list_sems, i, row_device(z, yy)))
+    def col_gather(buffer, sems, size, starts, pair):
+        def slot(p, w, t):
+            return buffer.at[pl.ds((p * 2 + w) * 16 + starts[t], size)]
+
+        return Gather(slot, x, zh, pair, col_device(ring(x, 1), zh), col_device(ring(x, -1), zh),
+                      sems.at[0], sems.at[1], pending)
+
+    gx = col_gather(xs, x_sems, 8, (0, 8), across)
+    x_across = x_ref.at[:, :, pl.ds(pl.multiple_of(lax.rem(r + 8, 16) * 128, 128), 128)]
+    for t in range(2):
+        for i in range(3):
+            gx.send(i, t, (x_src if i else x_across).at[pl.ds(8 * t, 8)])
+
     for i, (z, yy) in enumerate(row_peers):
         src = h_ref.at[:, :, pl.ds(pl.multiple_of((2 * yy + z) * 128, 128), 128)]
         panel_copies.append(remote(src, panels.at[pl.ds(chip * 8, 8)], panel_sems, i, row_device(z, yy)))
-
-    def col_gather(buffer, sems, size, starts, pair):
-        def slot(p, w, t):
-            return buffer.at[pl.ds((p * 2 + w) * 16 + starts[t], size)]
-
-        return Gather(slot, x, zh, pair, col_device(ring(x, 1), zh), col_device(ring(x, -1), zh),
-                      sems.at[0], sems.at[1], pending)
-
-    gx = col_gather(xs, x_sems, 16, (0,), across)
-    x_across = x_ref.at[:, :, pl.ds(pl.multiple_of(lax.rem(r + 8, 16) * 128, 128), 128)]
-    gx.send(0, 0, x_across)
-    gx.send(1, 0, x_src)
-    gx.send(2, 0, x_src)
 
     for copy in list_copies:
         copy.wait_recv()
@@ -150,133 +179,86 @@
     mine.wait()
     theirs.wait()
 
-    own_x.wait()
-    gx.wait(0)
-    gx.send(3)
-    gx.send(4)
-    gx.wait(1)
-    gx.send(5)
-
-    own_panel.wait()
-    for copy in panel_copies:
-        copy.wait_recv()
     pair_column = 4 * y + 2 * zl
-    lane = lax.broadcasted_iota(jnp.int32, (BLK, 128), 1)
-    line = lax.broadcasted_iota(jnp.int32, (BLK, 128), 0)
-    for side in range(2):
-        for s in range(K_NB):
-            i = index[pair_column + side, s]
-            local = jnp.where(lax.rem(i // 8, 2) == k, 8 * (i // 16) + lax.rem(i, 8), 64)
-            stack[s * BLK:(s + 1) * BLK, :] = panels[local]
-        pick = (lane == line + BLK * side).astype(jnp.bfloat16)
-        halves[side] = lax.dot_general(
-            pick, stack[...], (((1,), (1,)), ((), ())), preferred_element_type=jnp.float32
-        ).astype(jnp.bfloat16)
-    swap = remote(halves.at[1 - k], sib_half, half_sem, 0, sibling)
-    swap.wait_recv()
-    packed[pair_column + k] = halves[k] + sib_half[...]
-
-    def h_slot(p, w, t):
-        return packed.at[p * 4 + w * 2 + k]
+
+    def pack():
+        own_panel.wait()
+        for copy in panel_copies:
+            copy.wait_recv()
+        lane = lax.broadcasted_iota(jnp.int32, (BLK, 128), 1)
+        line = lax.broadcasted_iota(jnp.int32, (BLK, 128), 0)
+        for side in range(2):
+            blocks = []
+            for s in range(K_NB):
+                i = index[pair_column + side, s]
+                blocks.append(panels[jnp.where(lax.rem(i // 8, 2) == k, 8 * (i // 16) + lax.rem(i, 8), 64)])
+            pick = (lane == line + BLK * side).astype(jnp.bfloat16)
+            halves[side] = lax.dot_general(
+                pick, jnp.concatenate(blocks, axis=0), (((1,), (1,)), ((), ())), preferred_element_type=jnp.float32
+            ).astype(jnp.bfloat16)
+
+    swaps = []
+
+    def swap():
+        swaps.append(remote(halves.at[1 - k], sib_half, half_sem, 0, sibling))
+
+    def add():
+        swaps[0].wait_recv()
+        packed[pair_column + k] = halves[k] + sib_half[...]
 
     def row_gather(slot, sems):
         return Gather(slot, y, zl, row_device(1 - zl, y), row_device(zl, ring(y, 1)), row_device(zl, ring(y, -1)),
                       sems.at[0], sems.at[1], pending)
 
+    def h_slot(p, w, t):
+        return packed.at[p * 4 + w * 2 + k, pl.ds(32 * t, 32)]
+
     gh = row_gather(h_slot, h_sems)
     h_sib = {}
 
-    def pass_h(i):
-        slot = h_slot(y, zl, 0) if i == 0 else h_slot(*gh.received(i - 1), 0)
-        h_sib[i] = remote(slot, slot, h_sib_sems, i, sibling)
-
-    for i in range(3):
-        gh.send(i)
-    pass_h(0)
-
-    gx.wait(4)
-    gx.send(6)
-    for i in (2, 3, 5, 6):
-        gx.wait(i)
+    def pass_h(i, t):
+        place = (y, zl)
+        if i:
+            gh.need(i - 1, t)
+            place = gh.received(i - 1)
+        slot = h_slot(*place, t)
+        h_sib[i, t] = remote(slot, slot, h_sib_sems, 2 * i + t, sibling)
 
     def product(source, column):
         stacked = jnp.concatenate([source[index[column, s]] for s in range(K_NB)], axis=0)
         return jnp.dot(packed[column], stacked, preferred_element_type=jnp.float32)
 
     pairs = [gh.at(*d) for d in ((0, 0), (0, 1), (-1, 0), (1, 0), (1, 1), (-1, 1), (2, 0), (2, 1))]
+    passes = (0, 1, 2, 3, 5, 4, 6, 7)
     starts = [4 * p + 2 * w for p, w in pairs]
     across_z = col_device(x, 1 - zh)
     gs = col_gather(ss, s_sems, 2, starts, across_z)
 
-    def first_degree(t, sib):
-        h_sib[sib].wait_recv()
+    def first_degree(u):
+        if u == 0:
+            own_x.wait()
+            for t in range(2):
+                for i in range(7):
+                    gx.need(i, t)
+        for t in range(2):
+            if u:
+                gh.need(passes[u] - 1, t)
+            h_sib[passes[u], t].wait_recv()
         for j in range(2):
-            column = starts[t] + j
+            column = starts[u] + j
             at = c * 16 + column
             total = product(xs, column) - center_point * xs[at].astype(jnp.float32)
             ss[at] = (total / half_width).astype(jnp.bfloat16)
         for i in range(3):
-            gs.send(i, t)
-
-    def early(g, t):
-        g.wait(1, t)
-        g.send(5, t)
-        g.wait(0, t)
-        g.send(3, t)
-        g.send(4, t)
-
-    def late(g, t):
-        g.wait(4, t)
-        g.send(6, t)
-
-    def rest(g, t):
-        for i in (2, 3, 5, 6):
-            g.wait(i, t)
-
-    first_degree(0, 0)
-    gh.wait(0)
-    gh.send(3)
-    gh.send(4)
-    pass_h(1)
-    gh.wait(1)
-    gh.send(5)
-    pass_h(2)
-    gh.wait(2)
-    pass_h(3)
-    first_degree(1, 1)
-    first_degree(2, 2)
-    first_degree(3, 3)
-    early(gs, 0)
-    gh.wait(4)
-    gh.send(6)
-    pass_h(5)
-    early(gs, 1)
-    gh.wait(3)
-    pass_h(4)
-    early(gs, 2)
-    early(gs, 3)
-    first_degree(4, 5)
-    first_degree(5, 4)
-    late(gs, 0)
-    late(gs, 1)
-    gh.wait(5)
-    pass_h(6)
-    early(gs, 4)
-    early(gs, 5)
-    first_degree(6, 6)
-    gh.wait(6)
-    pass_h(7)
-    late(gs, 2)
-    late(gs, 3)
-    early(gs, 6)
-    first_degree(7, 7)
-    late(gs, 4)
-    late(gs, 5)
-    late(gs, 6)
-    early(gs, 7)
-    late(gs, 7)
+            gs.send(i, u)
+
+    does = {"x": gx.step, "pack": pack, "swap": swap, "add": add, "h": gh.step, "p": pass_h, "s": first_degree,
+            "g": gs.step}
+    for name, *args in FIRST:
+        does[name](*args)
     for t in range(8):
-        rest(gs, t)
+        for i in range(7):
+            gs.need(i, t)
 
     gf = col_gather(fs, f_sems, 4, (0, 4, 8, 12), across_z)
 
@@ -289,21 +271,27 @@
     gr = row_gather(r_slot(k), r_sems)
     r_sib = {}
 
-    def pass_r(i):
-        p, w = (y, zl) if i == 0 else gr.received(i - 1)
-        slot = rows.at[w * 8 + p * 2 + k]
-        r_sib[i] = remote(slot, slot, r_sib_sems, i, sibling)
-
     outs = []
 
-    def write_out(group, i):
+    def write_out(group):
         copy = pltpu.make_async_copy(
-            rows.at[group], f_ref.at[:, :, pl.ds(pl.multiple_of(group * 128, 128), 128)], out_sem.at[i]
+            rows.at[group], f_ref.at[:, :, pl.ds(pl.multiple_of(group * 128, 128), 128)], out_sem.at[len(outs)]
         )
         copy.start()
         outs.append(copy)
 
-    for t in range(4):
+    def pass_r(i):
+        place = (y, zl)
+        if i:
+            for t in range(4):
+                gr.need(i - 1, t)
+            place = gr.received(i - 1)
+        p, w = place
+        group = w * 8 + p * 2 + k
+        r_sib[i] = remote(rows.at[group], rows.at[group], r_sib_sems, i, sibling)
+        write_out(group)
+
+    def second_degree(t):
         for j in range(4):
             column = t * 4 + j
             at = c * 16 + column
@@ -314,37 +302,14 @@
         for i in (1, 2, 0):
             gf.send(i, t)
             gr.send(i, t)
-    pass_r(0)
-    for t in range(4):
-        early(gr, t)
-        early(gf, t)
-    pass_r(1)
-    pass_r(2)
-    for t in range(4):
-        gr.wait(2, t)
-    pass_r(3)
-    for t in range(4):
-        late(gr, t)
-        late(gf, t)
-    pass_r(5)
-    for t in range(4):
-        gr.wait(3, t)
-    pass_r(4)
-    places = [(y, zl)] + [gr.received(i) for i in range(7)]
-    for i, (p, w) in enumerate(places[:6]):
-        write_out(w * 8 + p * 2 + k, i)
-    for t in range(4):
-        gr.wait(5, t)
-    pass_r(6)
-    for t in range(4):
-        gr.wait(6, t)
-    pass_r(7)
-    for i in (6, 7):
-        p, w = places[i]
-        write_out(w * 8 + p * 2 + k, i)
-    for i, (p, w) in enumerate(places):
+
+    does = {"f": second_degree, "a": gf.step, "r": gr.step, "q": pass_r}
+    for name, *args in SECOND:
+        does[name](*args)
+    for i in range(8):
+        p, w = gr.received(i - 1) if i else (y, zl)
         r_sib[i].wait_recv()
-        write_out(w * 8 + p * 2 + 1 - k, 8 + i)
+        write_out(w * 8 + p * 2 + 1 - k)
 
     def project(which, left):
         def to(place, group):
@@ -366,7 +331,8 @@
 
     corr_copies = project(0, fs[pl.ds(c * 16, 16)].reshape(1024, 128))
     for t in range(4):
-        rest(gf, t)
+        for i in range(7):
+            gf.need(i, t)
 
     @pl.loop(0, 4)
     def _(j):
@@ -415,7 +381,6 @@
             vmem((128, BLK, 128), bf16),
             vmem((16, 16, BLK, 128), bf16),
             vmem((16, BLK, 128), bf16),
-            vmem((DEPTH, 128), bf16),
             vmem((8, K_NB), jnp.int32),
             vmem((2, 8, 128, 256), bf16),
             vmem((2, 8, 128, 256), bf16),
@@ -425,9 +390,9 @@
             dma((2, 1)),
             dma((2,)),
             dma((2, 1)),
-            dma((2, 7, 1)),
-            dma((2, 8)),
-            dma((2, 7, 1)),
+            dma((2, 7, 2)),
+            dma((2, 16)),
+            dma((2, 7, 2)),
             dma((2, 7, 8)),
             dma((2, 7, 4)),
             dma((2, 7, 4)),
@@ -436,15 +401,12 @@
             dma((16,)),
         ],
         compiler_params=pltpu.CompilerParams(
-            collective_id=0, has_side_effects=True, vmem_limit_bytes=62 * 1024 * 1024
+            collective_id=0, has_side_effects=True, vmem_limit_bytes=48 * 1024 * 1024
         ),
     )(hamiltonian.reshape(8, BLK, 1024), block_cols, start_vectors.reshape(16, BLK, 2048))
 
     def hand_on(*refs):
-        sources, targets, sems = refs[:3], refs[3:6], refs[6]
-        copies = [pltpu.make_async_copy(a.at[4 * i:4 * i + 4], b.at[4 * i:4 * i + 4], sems.at[i])
-                  for a, b in (refs[0:4:3],) for i in range(4)]
-        copies += [pltpu.make_async_copy(sources[i], targets[i], sems.at[3 + i]) for i in (1, 2)]
+        copies = [pltpu.make_async_copy(refs[i], refs[3 + i], refs[6].at[i]) for i in range(3)]
         for copy in copies:
             copy.start()
         for copy in copies:
@@ -455,8 +417,8 @@
         out_shape=out_shape,
         in_specs=[place] * 3,
         out_specs=(place,) * 3,
-        scratch_shapes=[dma((6,))],
-        compiler_params=pltpu.CompilerParams(vmem_limit_bytes=62 * 1024 * 1024),
+        scratch_shapes=[dma((3,))],
+        compiler_params=pltpu.CompilerParams(vmem_limit_bytes=40 * 1024 * 1024),
     )(*results)
     return f.reshape(1024, 2048), corr, proj
 

time: 239 us -> 103 us (0.43)
  Pallas kernels: 238 us -> 100 us
    pallas_call x1, Pallas kernels: 136 us -> 2.1 us  [shards(): pl.pallas_call(hand_on, out_shape=out_shape, in_specs=[place] * 3, out_sp...]
    pallas_call x1, Pallas kernels: 102 us -> 97.9 us  [shards(): pl.pallas_call(kernel, out_shape=out_shape, in_specs=[place] * 3, out_spe...]
where the time goes in v3:
time: 103 us
  Pallas kernels  100 us (97%)
  local copies, waits for them, and re-layouts  1.9 us (2%)
    pallas_call x1, Pallas kernels, shards(): pl.pallas_call(kernel, out_shape=out_shape, in_specs=[place] * 3, out_spe...  97.9 us
    pallas_call x1, Pallas kernels, shards(): pl.pallas_call(hand_on, out_shape=out_shape, in_specs=[place] * 3, out_sp...  2.1 us

profile of v3, /device:TPU:1, one launch (start us, length us, event | category | flops | bytes accessed | tf_op | source)
XLA Modules:
  0.0 102.5 jit_solution(10314914289395746169)
XLA Ops:
  0.6 0.0 copy-start
  0.6 1.2 %copy-done = bf16[512,1024]{1,0:T(8,128)(2,1)S(1)} copy-done((bf16[512,1024]{1,0:T(8,128)(2,1)S(1)}, bf16[512,1024]{1,0:T(8,128)(2,1)}, u32[]{:S(2)}) %copy-start) | copy-done | bytes 1048600
  1.9 0.0 copy-start.1
  1.9 0.7 copy-done.1
  2.5 97.9 %shard_map.58 = (bf16[16,64,2048]{2,1,0:T(8,128)(2,1)S(1)}, f32[128,256]{1,0:T(8,128)S(1)}, f32[128,256]{1,0:T(8,128)S(1)}) custom-call(bf16[8,64,1024]{2,1,0:T(8,128)(2,1)S(1)} %bitcast.3, s32[8,26]{1,0:T(8,128)S(1)} %copy-done.1, bf16[16,64,2048]{2,1,0:T(8,128)(2,1)} %bitcast.4), custom_call_target="tpu_custom_call" | custom-call | tf_op jit(solution)/shard_map/pallas_call | solution.py:366
  100.4 2.1 %shard_map.59 = (bf16[16,64,2048]{2,1,0:T(8,128)(2,1)}, f32[128,256]{1,0:T(8,128)}, f32[128,256]{1,0:T(8,128)}) custom-call(bf16[16,64,2048]{2,1,0:T(8,128)(2,1)S(1)} %get-tuple-element.9.refs_0_, f32[128,256]{1,0:T(8,128)S(1)} %get-tuple-element.10.refs_1_, f32[128,256]{1,0:T(8,128)S(1)} %get-tuple-element.11.refs_2_), custom_call_target="tpu_custom_call" | custom-call | tf_op jit(solution)/shard_map/pallas_call | solution.py:415
Async XLA Ops:
  0.6 1.2 %copy-start = (bf16[512,1024]{1,0:T(8,128)(2,1)S(1)}, bf16[512,1024]{1,0:T(8,128)(2,1)}, u32[]{:S(2)}) copy-start(bf16[512,1024]{1,0:T(8,128)(2,1)} %param.3) | copy-start | bytes 3145732
  1.9 0.7 copy-start.1

commit v4 on v3

--- a/solution.py
+++ b/solution.py
@@ -12,17 +12,28 @@
 center_point = 0.2
 half_width = 0.8
 
+FORWARD = (((0, 0), "P"), ((0, 0), "R"), ((0, 0), "L"), ((0, 1), "R"),
+           ((0, 1), "L"), ((-1, 0), "R"), ((1, 1), "L"))
+PAIR_LAST_RIGHT = (((0, 0), "P"), ((0, 0), "R"), ((0, 0), "L"), ((-1, 0), "P"),
+                   ((1, 0), "P"), ((-1, 0), "R"), ((2, 0), "P"))
+PAIR_LAST_DIRECT = (((0, 0), "P"), ((0, 0), "R"), ((0, 0), "L"), ((-1, 0), "P"),
+                    ((1, 0), "P"), ((0, 0), "X"), ((2, 0), "P"))
+DIRECT = (((0, 0), "P"), ((0, 0), "R"), ((0, 0), "L"), ((0, 1), "R"),
+          ((0, 1), "L"), ((0, 0), "X"), ((0, 1), "X"))
+S_MESSAGES = (DIRECT, FORWARD, PAIR_LAST_DIRECT, FORWARD, PAIR_LAST_RIGHT, FORWARD, PAIR_LAST_DIRECT, DIRECT)
+F_MESSAGES = (FORWARD, FORWARD, FORWARD, FORWARD)
+ROW_MESSAGES = (FORWARD, FORWARD, FORWARD, FORWARD)
+SLOTS = ((0, 0), (0, 1), (-1, 0), (1, 0), (-1, 1), (1, 1), (2, 0), (2, 1))
 FIRST = (
-    ("x", 5, 0), ("x", 3, 0), ("x", 4, 0), ("x", 5, 1), ("x", 3, 1), ("x", 4, 1), ("pack",), ("swap",), ("x", 6, 0),
-    ("add",), ("h", 0, 0), ("h", 1, 0), ("h", 2, 0), ("p", 0, 0), ("h", 0, 1), ("h", 1, 1), ("h", 2, 1), ("p", 0, 1),
+    ("x", 5, 0), ("x", 3, 0), ("x", 4, 0), ("x", 5, 1), ("x", 3, 1), ("x", 4, 1), ("pack",), ("x", 6, 0), ("add",),
+    ("h", 0, 0), ("h", 1, 0), ("h", 2, 0), ("p", 0, 0), ("h", 0, 1), ("h", 1, 1), ("h", 2, 1), ("p", 0, 1),
     ("x", 6, 1), ("h", 3, 0), ("h", 4, 0), ("p", 1, 0), ("h", 5, 0), ("p", 2, 0), ("p", 3, 0), ("h", 3, 1),
-    ("h", 4, 1), ("p", 1, 1), ("h", 5, 1), ("p", 2, 1), ("p", 3, 1), ("s", 0), ("g", 5, 0), ("s", 1), ("g", 3, 0),
-    ("g", 4, 0), ("p", 4, 0), ("h", 6, 0), ("p", 5, 0), ("s", 2), ("s", 3), ("p", 6, 0), ("h", 6, 1), ("p", 5, 1),
-    ("g", 5, 1), ("g", 3, 1), ("g", 4, 1), ("g", 6, 0), ("g", 5, 2), ("s", 4), ("g", 3, 2), ("g", 4, 2), ("p", 4, 1),
-    ("p", 7, 0), ("g", 5, 3), ("g", 3, 3), ("g", 4, 3), ("g", 6, 1), ("s", 5), ("g", 6, 2), ("p", 6, 1), ("p", 7, 1),
-    ("g", 3, 4), ("g", 4, 4), ("g", 5, 4), ("s", 6), ("g", 6, 3), ("s", 7), ("g", 3, 5), ("g", 4, 5), ("g", 5, 5),
-    ("g", 6, 4), ("g", 3, 6), ("g", 4, 6), ("g", 5, 6), ("g", 3, 7), ("g", 4, 7), ("g", 5, 7), ("g", 6, 5),
-    ("g", 6, 6), ("g", 6, 7),
+    ("h", 4, 1), ("p", 1, 1), ("h", 5, 1), ("p", 2, 1), ("p", 3, 1), ("s", 0), ("s", 1), ("g", 3, 0), ("g", 4, 0),
+    ("p", 4, 0), ("h", 6, 0), ("p", 5, 0), ("g", 6, 0), ("s", 2), ("s", 3), ("g", 5, 1), ("p", 6, 0), ("h", 6, 1),
+    ("p", 5, 1), ("g", 3, 1), ("g", 4, 1), ("s", 4), ("g", 3, 2), ("p", 4, 1), ("p", 7, 0), ("g", 4, 2), ("g", 3, 3),
+    ("g", 4, 3), ("g", 6, 2), ("g", 5, 3), ("s", 5), ("g", 6, 1), ("p", 6, 1), ("p", 7, 1), ("g", 4, 4), ("g", 6, 3),
+    ("g", 3, 4), ("g", 5, 4), ("s", 6), ("s", 7), ("g", 5, 5), ("g", 3, 5), ("g", 4, 5), ("g", 6, 4), ("g", 4, 6),
+    ("g", 3, 6), ("g", 6, 6), ("g", 3, 7), ("g", 4, 7), ("g", 6, 7), ("g", 6, 5),
 )
 SECOND = (
     ("f", 0), ("f", 1), ("f", 2), ("f", 3), ("q", 0), ("r", 5, 0), ("r", 3, 0), ("r", 4, 0), ("a", 5, 0), ("a", 3, 0),
@@ -33,54 +44,62 @@
 )
 
 
+def same(slot):
+    return slot[0] % 4, slot[1] % 2
+
+
+def comes(message):
+    (dp, dw), to = message
+    return same({"P": (dp, dw + 1), "R": (dp - 1, dw), "L": (dp + 1, dw), "X": (dp + 2, dw)}[to])
+
+
 class Gather:
-    def __init__(self, slot, p, w, pair, right, left, send_sem, recv_sem, pending):
-        self.slot, self.p, self.w = slot, p, w
-        self.pair, self.right, self.left = pair, right, left
-        self.send_sem, self.recv_sem, self.pending = send_sem, recv_sem, pending
+    def __init__(self, slot, p, w, devices, sems, pending, messages):
+        self.slot, self.p, self.w, self.devices = slot, p, w, devices
+        self.send_sem, self.recv_sem, self.pending = sems.at[0], sems.at[1], pending
+        self.messages = messages
         self.waited = set()
 
     def at(self, dp, dw):
         return lax.rem(self.p + dp + 4, 4), (self.w + dw) % 2
 
-    def sent(self, i):
-        return self.at(*((0, 0), (0, 0), (0, 0), (0, 1), (0, 1), (-1, 0), (1, 1))[i])
-
-    def received(self, i):
-        return self.at(*((0, 1), (-1, 0), (1, 0), (-1, 1), (1, 1), (2, 0), (2, 1))[i])
-
-    def send(self, i, chunk=0, src=None):
-        dst = self.slot(*self.sent(i), chunk)
-        to = self.pair if i == 0 else (self.right if i % 2 else self.left)
-        copy = pltpu.make_async_remote_copy(
-            src_ref=dst if src is None else src,
-            dst_ref=dst,
-            send_sem=self.send_sem.at[i, chunk],
-            recv_sem=self.recv_sem.at[i, chunk],
-            device_id=to,
-            device_id_type=MESH,
-        )
-        copy.start()
-        self.pending.append(copy)
-
-    def need(self, i, chunk=0):
-        if (i, chunk) in self.waited:
-            return
-        self.waited.add((i, chunk))
-        ref = self.slot(*self.received(i), chunk)
-        pltpu.make_async_remote_copy(
-            src_ref=ref,
+    def copy(self, ref, src, i, chunk):
+        return pltpu.make_async_remote_copy(
+            src_ref=src,
             dst_ref=ref,
             send_sem=self.send_sem.at[i, chunk],
             recv_sem=self.recv_sem.at[i, chunk],
-            device_id=self.pair,
+            device_id=self.devices[self.messages[chunk][i][1]],
             device_id_type=MESH,
-        ).wait_recv()
-
-    def step(self, i, chunk=0):
-        if i >= 3:
-            self.need((0, 0, 1, 4)[i - 3], chunk)
-        self.send(i, chunk)
+        )
+
+    def carrier(self, slot, chunk):
+        brings = [comes(message) for message in self.messages[chunk]]
+        return None if same(slot) == (0, 0) else brings.index(same(slot))
+
+    def need(self, slot, chunk=0):
+        i = self.carrier(slot, chunk)
+        if i is not None and (i, chunk) not in self.waited:
+            self.waited.add((i, chunk))
+            ref = self.slot(*self.at(*slot), chunk)
+            self.copy(ref, ref, i, chunk).wait_recv()
+        return self.at(*slot)
+
+    def need_all(self):
+        for chunk in range(len(self.messages)):
+            for slot in SLOTS:
+                self.need(slot, chunk)
+
+    def own(self, chunk=0, sources=None):
+        for i, (slot, to) in enumerate(self.messages[chunk]):
+            if slot == (0, 0):
+                self.step(i, chunk, sources and sources[to])
+
+    def step(self, i, chunk=0, src=None):
+        dst = self.slot(*self.need(self.messages[chunk][i][0], chunk), chunk)
+        copy = self.copy(dst, dst if src is None else src, i, chunk)
+        copy.start()
+        self.pending.append(copy)
 
 
 def kernel(
@@ -133,9 +152,6 @@
     own_x.start()
     read_lists = pltpu.make_async_copy(lists_ref, own_lists, own_sem.at[2])
     read_lists.start()
-    read_lists.wait()
-    lists[chip] = jnp.zeros((8, 128), jnp.int32)
-    lists[chip, :, :K_NB] = own_lists[...]
     panels[64] = jnp.zeros((BLK, 128), jnp.bfloat16)
 
     barrier = pltpu.get_barrier_semaphore()
@@ -146,23 +162,27 @@
     across = (lax.rem(r + 8, 16), x * 2 + 1 - zh)
     for device in (sibling, across):
         pl.semaphore_signal(barrier, inc=1, device_id=device, device_id_type=MESH)
+    read_lists.wait()
+    lists[chip] = jnp.zeros((8, 128), jnp.int32)
+    lists[chip, :, :K_NB] = own_lists[...]
     pl.semaphore_wait(barrier, 16)
 
     list_copies, panel_copies = [], []
     for i, (z, yy) in enumerate(row_peers):
         list_copies.append(remote(lists.at[chip], lists.at[chip], list_sems, i, row_device(z, yy)))
-    def col_gather(buffer, sems, size, starts, pair):
+    def col_gather(buffer, sems, size, starts, pair, messages):
         def slot(p, w, t):
             return buffer.at[pl.ds((p * 2 + w) * 16 + starts[t], size)]
 
-        return Gather(slot, x, zh, pair, col_device(ring(x, 1), zh), col_device(ring(x, -1), zh),
-                      sems.at[0], sems.at[1], pending)
-
-    gx = col_gather(xs, x_sems, 8, (0, 8), across)
+        devices = {"P": pair, "R": col_device(ring(x, 1), zh), "L": col_device(ring(x, -1), zh),
+                   "X": col_device(ring(x, 2), zh)}
+        return Gather(slot, x, zh, devices, sems, pending, messages)
+
+    gx = col_gather(xs, x_sems, 8, (0, 8), across, (FORWARD,) * 2)
     x_across = x_ref.at[:, :, pl.ds(pl.multiple_of(lax.rem(r + 8, 16) * 128, 128), 128)]
     for t in range(2):
-        for i in range(3):
-            gx.send(i, t, (x_src if i else x_across).at[pl.ds(8 * t, 8)])
+        half = pl.ds(8 * t, 8)
+        gx.own(t, {"P": x_across.at[half], "R": x_src.at[half], "L": x_src.at[half]})
 
     for i, (z, yy) in enumerate(row_peers):
         src = h_ref.at[:, :, pl.ds(pl.multiple_of((2 * yy + z) * 128, 128), 128)]
@@ -181,86 +201,77 @@
 
     pair_column = 4 * y + 2 * zl
 
+    def pack_side(side):
+        lane = lax.broadcasted_iota(jnp.int32, (BLK, 128), 1)
+        line = lax.broadcasted_iota(jnp.int32, (BLK, 128), 0)
+        blocks = []
+        for s in range(K_NB):
+            i = index[pair_column + side, s]
+            blocks.append(panels[jnp.where(lax.rem(i // 8, 2) == k, 8 * (i // 16) + lax.rem(i, 8), 64)])
+        pick = (lane == line + BLK * side).astype(jnp.bfloat16)
+        return lax.dot_general(
+            pick, jnp.concatenate(blocks, axis=0), (((1,), (1,)), ((), ())), preferred_element_type=jnp.float32
+        ).astype(jnp.bfloat16)
+
+    swaps = []
+
     def pack():
         own_panel.wait()
         for copy in panel_copies:
             copy.wait_recv()
-        lane = lax.broadcasted_iota(jnp.int32, (BLK, 128), 1)
-        line = lax.broadcasted_iota(jnp.int32, (BLK, 128), 0)
-        for side in range(2):
-            blocks = []
-            for s in range(K_NB):
-                i = index[pair_column + side, s]
-                blocks.append(panels[jnp.where(lax.rem(i // 8, 2) == k, 8 * (i // 16) + lax.rem(i, 8), 64)])
-            pick = (lane == line + BLK * side).astype(jnp.bfloat16)
-            halves[side] = lax.dot_general(
-                pick, jnp.concatenate(blocks, axis=0), (((1,), (1,)), ((), ())), preferred_element_type=jnp.float32
-            ).astype(jnp.bfloat16)
-
-    swaps = []
-
-    def swap():
-        swaps.append(remote(halves.at[1 - k], sib_half, half_sem, 0, sibling))
+        halves[0] = pack_side(1 - k)
+        swaps.append(remote(halves.at[0], sib_half, half_sem, 0, sibling))
+        halves[1] = pack_side(k)
 
     def add():
         swaps[0].wait_recv()
-        packed[pair_column + k] = halves[k] + sib_half[...]
-
-    def row_gather(slot, sems):
-        return Gather(slot, y, zl, row_device(1 - zl, y), row_device(zl, ring(y, 1)), row_device(zl, ring(y, -1)),
-                      sems.at[0], sems.at[1], pending)
+        packed[pair_column + k] = halves[1] + sib_half[...]
+
+    def row_gather(slot, sems, messages):
+        devices = {"P": row_device(1 - zl, y), "R": row_device(zl, ring(y, 1)), "L": row_device(zl, ring(y, -1)),
+                   "X": row_device(zl, ring(y, 2))}
+        return Gather(slot, y, zl, devices, sems, pending, messages)
 
     def h_slot(p, w, t):
         return packed.at[p * 4 + w * 2 + k, pl.ds(32 * t, 32)]
 
-    gh = row_gather(h_slot, h_sems)
+    gh = row_gather(h_slot, h_sems, (FORWARD,) * 2)
     h_sib = {}
 
     def pass_h(i, t):
-        place = (y, zl)
-        if i:
-            gh.need(i - 1, t)
-            place = gh.received(i - 1)
-        slot = h_slot(*place, t)
+        slot = h_slot(*gh.need(SLOTS[i], t), t)
         h_sib[i, t] = remote(slot, slot, h_sib_sems, 2 * i + t, sibling)
 
     def product(source, column):
         stacked = jnp.concatenate([source[index[column, s]] for s in range(K_NB)], axis=0)
         return jnp.dot(packed[column], stacked, preferred_element_type=jnp.float32)
 
-    pairs = [gh.at(*d) for d in ((0, 0), (0, 1), (-1, 0), (1, 0), (1, 1), (-1, 1), (2, 0), (2, 1))]
     passes = (0, 1, 2, 3, 5, 4, 6, 7)
-    starts = [4 * p + 2 * w for p, w in pairs]
+    starts = [4 * p + 2 * w for p, w in (gh.at(*SLOTS[i]) for i in passes)]
     across_z = col_device(x, 1 - zh)
-    gs = col_gather(ss, s_sems, 2, starts, across_z)
+    gs = col_gather(ss, s_sems, 2, starts, across_z, S_MESSAGES)
 
     def first_degree(u):
         if u == 0:
             own_x.wait()
-            for t in range(2):
-                for i in range(7):
-                    gx.need(i, t)
+            gx.need_all()
         for t in range(2):
-            if u:
-                gh.need(passes[u] - 1, t)
+            gh.need(SLOTS[passes[u]], t)
             h_sib[passes[u], t].wait_recv()
         for j in range(2):
             column = starts[u] + j
             at = c * 16 + column
             total = product(xs, column) - center_point * xs[at].astype(jnp.float32)
             ss[at] = (total / half_width).astype(jnp.bfloat16)
-        for i in range(3):
-            gs.send(i, u)
-
-    does = {"x": gx.step, "pack": pack, "swap": swap, "add": add, "h": gh.step, "p": pass_h, "s": first_degree,
+        gs.own(u)
+
+    does = {"x": gx.step, "pack": pack, "add": add, "h": gh.step, "p": pass_h, "s": first_degree,
             "g": gs.step}
     for name, *args in FIRST:
         does[name](*args)
-    for t in range(8):
-        for i in range(7):
-            gs.need(i, t)
-
-    gf = col_gather(fs, f_sems, 4, (0, 4, 8, 12), across_z)
+    gs.need_all()
+
+    gf = col_gather(fs, f_sems, 4, (0, 4, 8, 12), across_z, F_MESSAGES)
 
     def r_slot(parity):
         def slot(p, w, t):
@@ -268,7 +279,7 @@
 
         return slot
 
-    gr = row_gather(r_slot(k), r_sems)
+    gr = row_gather(r_slot(k), r_sems, ROW_MESSAGES)
     r_sib = {}
 
     outs = []
@@ -281,12 +292,8 @@
         outs.append(copy)
 
     def pass_r(i):
-        place = (y, zl)
-        if i:
-            for t in range(4):
-                gr.need(i - 1, t)
-            place = gr.received(i - 1)
-        p, w = place
+        for t in range(4):
+            p, w = gr.need(SLOTS[i], t)
         group = w * 8 + p * 2 + k
         r_sib[i] = remote(rows.at[group], rows.at[group], r_sib_sems, i, sibling)
         write_out(group)
@@ -299,15 +306,14 @@
             out = ((2.0 / half_width) * total - xs[at].astype(jnp.float32)).astype(jnp.bfloat16)
             fs[at] = out
             rows[r, column] = out
-        for i in (1, 2, 0):
-            gf.send(i, t)
-            gr.send(i, t)
+        gf.own(t)
+        gr.own(t)
 
     does = {"f": second_degree, "a": gf.step, "r": gr.step, "q": pass_r}
     for name, *args in SECOND:
         does[name](*args)
     for i in range(8):
-        p, w = gr.received(i - 1) if i else (y, zl)
+        p, w = gr.at(*SLOTS[i])
         r_sib[i].wait_recv()
         write_out(w * 8 + p * 2 + 1 - k)
 
@@ -330,9 +336,7 @@
         return copies
 
     corr_copies = project(0, fs[pl.ds(c * 16, 16)].reshape(1024, 128))
-    for t in range(4):
-        for i in range(7):
-            gf.need(i, t)
+    gf.need_all()
 
     @pl.loop(0, 4)
     def _(j):
@@ -342,15 +346,17 @@
 
     proj_copies = project(1, image[...].reshape(1024, 128))
 
+    for copy in pending[:-14]:
+        copy.wait_send()
+    for copy in outs:
+        copy.wait()
     for copy in corr_copies:
         copy.wait_recv()
     corr_ref[...] = jnp.sum(parts[0].astype(jnp.float32), axis=0) / 8192.0
     for copy in proj_copies:
         copy.wait_recv()
     proj_ref[...] = jnp.sum(parts[1].astype(jnp.float32), axis=0) / 8192.0
-    for copy in outs:
-        copy.wait()
-    for copy in pending:
+    for copy in corr_copies + proj_copies:
         copy.wait_send()
 
 
@@ -406,7 +412,10 @@
     )(hamiltonian.reshape(8, BLK, 1024), block_cols, start_vectors.reshape(16, BLK, 2048))
 
     def hand_on(*refs):
-        copies = [pltpu.make_async_copy(refs[i], refs[3 + i], refs[6].at[i]) for i in range(3)]
+        copies = [pltpu.make_async_copy(refs[i], refs[3 + i], refs[6].at[i]) for i in (1, 2)]
+        for i in range(4):
+            part = pl.ds(4 * i, 4)
+            copies.append(pltpu.make_async_copy(refs[0].at[part], refs[3].at[part], refs[6].at[3 + i]))
         for copy in copies:
             copy.start()
         for copy in copies:
@@ -417,7 +426,7 @@
         out_shape=out_shape,
         in_specs=[place] * 3,
         out_specs=(place,) * 3,
-        scratch_shapes=[dma((3,))],
+        scratch_shapes=[dma((7,))],
         compiler_params=pltpu.CompilerParams(vmem_limit_bytes=40 * 1024 * 1024),
     )(*results)
     return f.reshape(1024, 2048), corr, proj

time: 103 us -> 99.9 us (0.970)
  Pallas kernels: 100 us -> 97.1 us
    pallas_call x1, Pallas kernels: 97.9 us -> 95 us  [shards(): pl.pallas_call(kernel, out_shape=out_shape, in_specs=[place] * 3, out_spe...]
where the time goes in v4:
time: 99.9 us; the launch traced here: 99.7 us
  Pallas kernels  97.1 us (97%)
  local copies, waits for them, and re-layouts  1.9 us (2%)
    pallas_call x1, Pallas kernels, shards(): pl.pallas_call(kernel, out_shape=out_shape, in_specs=[place] * 3, out_spe...  95 us
    pallas_call x1, Pallas kernels, shards(): pl.pallas_call(hand_on, out_shape=out_shape, in_specs=[place] * 3, out_sp...  2.15 us

profile of v4, /device:TPU:1, one launch (start us, length us, event | category | flops | bytes accessed | tf_op | source)
XLA Modules:
  0.0 99.7 jit_solution(2729545460377516325)
XLA Ops:
  0.6 0.0 copy-start
  0.6 1.2 %copy-done = bf16[512,1024]{1,0:T(8,128)(2,1)S(1)} copy-done((bf16[512,1024]{1,0:T(8,128)(2,1)S(1)}, bf16[512,1024]{1,0:T(8,128)(2,1)}, u32[]{:S(2)}) %copy-start) | copy-done | bytes 1048600
  1.9 0.0 copy-start.1
  1.9 0.7 copy-done.1
  2.5 95.0 %shard_map.58 = (bf16[16,64,2048]{2,1,0:T(8,128)(2,1)S(1)}, f32[128,256]{1,0:T(8,128)S(1)}, f32[128,256]{1,0:T(8,128)S(1)}) custom-call(bf16[8,64,1024]{2,1,0:T(8,128)(2,1)S(1)} %bitcast.3, s32[8,26]{1,0:T(8,128)S(1)} %copy-done.1, bf16[16,64,2048]{2,1,0:T(8,128)(2,1)} %bitcast.4), custom_call_target="tpu_custom_call" | custom-call | tf_op jit(solution)/shard_map/pallas_call | solution.py:372
  97.5 2.2 %shard_map.59 = (bf16[16,64,2048]{2,1,0:T(8,128)(2,1)}, f32[128,256]{1,0:T(8,128)}, f32[128,256]{1,0:T(8,128)}) custom-call(bf16[16,64,2048]{2,1,0:T(8,128)(2,1)S(1)} %get-tuple-element.9.refs_0_, f32[128,256]{1,0:T(8,128)S(1)} %get-tuple-element.10.refs_1_, f32[128,256]{1,0:T(8,128)S(1)} %get-tuple-element.11.refs_2_), custom_call_target="tpu_custom_call" | custom-call | tf_op jit(solution)/shard_map/pallas_call | solution.py:424
Async XLA Ops:
  0.6 1.2 %copy-start = (bf16[512,1024]{1,0:T(8,128)(2,1)S(1)}, bf16[512,1024]{1,0:T(8,128)(2,1)}, u32[]{:S(2)}) copy-start(bf16[512,1024]{1,0:T(8,128)(2,1)} %param.3) | copy-start | bytes 3145732
  1.9 0.7 copy-start.1

commit v5 on v4

--- a/solution.py
+++ b/solution.py
@@ -16,11 +16,13 @@
            ((0, 1), "L"), ((-1, 0), "R"), ((1, 1), "L"))
 PAIR_LAST_RIGHT = (((0, 0), "P"), ((0, 0), "R"), ((0, 0), "L"), ((-1, 0), "P"),
                    ((1, 0), "P"), ((-1, 0), "R"), ((2, 0), "P"))
+PAIR_LAST_LEFT = (((0, 0), "P"), ((0, 0), "R"), ((0, 0), "L"), ((-1, 0), "P"),
+                  ((1, 0), "P"), ((1, 0), "L"), ((2, 0), "P"))
 PAIR_LAST_DIRECT = (((0, 0), "P"), ((0, 0), "R"), ((0, 0), "L"), ((-1, 0), "P"),
                     ((1, 0), "P"), ((0, 0), "X"), ((2, 0), "P"))
 DIRECT = (((0, 0), "P"), ((0, 0), "R"), ((0, 0), "L"), ((0, 1), "R"),
           ((0, 1), "L"), ((0, 0), "X"), ((0, 1), "X"))
-S_MESSAGES = (DIRECT, FORWARD, PAIR_LAST_DIRECT, FORWARD, PAIR_LAST_RIGHT, FORWARD, PAIR_LAST_DIRECT, DIRECT)
+S_MESSAGES = (DIRECT, PAIR_LAST_LEFT, PAIR_LAST_LEFT, FORWARD, PAIR_LAST_RIGHT, FORWARD, PAIR_LAST_DIRECT, DIRECT)
 F_MESSAGES = (FORWARD, FORWARD, FORWARD, FORWARD)
 ROW_MESSAGES = (FORWARD, FORWARD, FORWARD, FORWARD)
 SLOTS = ((0, 0), (0, 1), (-1, 0), (1, 0), (-1, 1), (1, 1), (2, 0), (2, 1))
@@ -29,11 +31,11 @@
     ("h", 0, 0), ("h", 1, 0), ("h", 2, 0), ("p", 0, 0), ("h", 0, 1), ("h", 1, 1), ("h", 2, 1), ("p", 0, 1),
     ("x", 6, 1), ("h", 3, 0), ("h", 4, 0), ("p", 1, 0), ("h", 5, 0), ("p", 2, 0), ("p", 3, 0), ("h", 3, 1),
     ("h", 4, 1), ("p", 1, 1), ("h", 5, 1), ("p", 2, 1), ("p", 3, 1), ("s", 0), ("s", 1), ("g", 3, 0), ("g", 4, 0),
-    ("p", 4, 0), ("h", 6, 0), ("p", 5, 0), ("g", 6, 0), ("s", 2), ("s", 3), ("g", 5, 1), ("p", 6, 0), ("h", 6, 1),
-    ("p", 5, 1), ("g", 3, 1), ("g", 4, 1), ("s", 4), ("g", 3, 2), ("p", 4, 1), ("p", 7, 0), ("g", 4, 2), ("g", 3, 3),
-    ("g", 4, 3), ("g", 6, 2), ("g", 5, 3), ("s", 5), ("g", 6, 1), ("p", 6, 1), ("p", 7, 1), ("g", 4, 4), ("g", 6, 3),
-    ("g", 3, 4), ("g", 5, 4), ("s", 6), ("s", 7), ("g", 5, 5), ("g", 3, 5), ("g", 4, 5), ("g", 6, 4), ("g", 4, 6),
-    ("g", 3, 6), ("g", 6, 6), ("g", 3, 7), ("g", 4, 7), ("g", 6, 7), ("g", 6, 5),
+    ("p", 4, 0), ("h", 6, 0), ("p", 5, 0), ("g", 6, 0), ("s", 2), ("s", 3), ("g", 3, 1), ("g", 4, 1), ("p", 6, 0),
+    ("h", 6, 1), ("p", 5, 1), ("g", 5, 1), ("s", 4), ("g", 3, 2), ("p", 4, 1), ("p", 7, 0), ("g", 4, 2), ("g", 5, 2),
+    ("g", 3, 3), ("g", 4, 3), ("g", 5, 3), ("g", 6, 1), ("s", 5), ("p", 6, 1), ("g", 3, 4), ("p", 7, 1), ("g", 5, 4),
+    ("g", 4, 4), ("g", 6, 2), ("s", 6), ("g", 6, 3), ("s", 7), ("g", 5, 5), ("g", 6, 4), ("g", 3, 5), ("g", 4, 5),
+    ("g", 3, 6), ("g", 4, 6), ("g", 6, 6), ("g", 3, 7), ("g", 4, 7), ("g", 6, 7), ("g", 6, 5),
 )
 SECOND = (
     ("f", 0), ("f", 1), ("f", 2), ("f", 3), ("q", 0), ("r", 5, 0), ("r", 3, 0), ("r", 4, 0), ("a", 5, 0), ("a", 3, 0),

time: 99.9 us -> 99.5 us (level)
  no operation moved by 1% of the time
where the time goes in v5:
time: 99.5 us; the launch traced here: 99.3 us
  Pallas kernels  96.7 us (97%)
  local copies, waits for them, and re-layouts  1.9 us (2%)
    pallas_call x1, Pallas kernels, shards(): pl.pallas_call(kernel, out_shape=out_shape, in_specs=[place] * 3, out_spe...  94.6 us
    pallas_call x1, Pallas kernels, shards(): pl.pallas_call(hand_on, out_shape=out_shape, in_specs=[place] * 3, out_sp...  2.15 us

profile of v5, /device:TPU:1, one launch (start us, length us, event | category | flops | bytes accessed | tf_op | source)
XLA Modules:
  0.0 99.3 jit_solution(10492740516605278091)
XLA Ops:
  0.6 0.0 copy-start
  0.6 1.2 %copy-done = bf16[512,1024]{1,0:T(8,128)(2,1)S(1)} copy-done((bf16[512,1024]{1,0:T(8,128)(2,1)S(1)}, bf16[512,1024]{1,0:T(8,128)(2,1)}, u32[]{:S(2)}) %copy-start) | copy-done | bytes 1048600
  1.9 0.0 copy-start.1
  1.9 0.7 copy-done.1
  2.5 94.6 %shard_map.58 = (bf16[16,64,2048]{2,1,0:T(8,128)(2,1)S(1)}, f32[128,256]{1,0:T(8,128)S(1)}, f32[128,256]{1,0:T(8,128)S(1)}) custom-call(bf16[8,64,1024]{2,1,0:T(8,128)(2,1)S(1)} %bitcast.3, s32[8,26]{1,0:T(8,128)S(1)} %copy-done.1, bf16[16,64,2048]{2,1,0:T(8,128)(2,1)} %bitcast.4), custom_call_target="tpu_custom_call" | custom-call | tf_op jit(solution)/shard_map/pallas_call | solution.py:374
  97.1 2.2 %shard_map.59 = (bf16[16,64,2048]{2,1,0:T(8,128)(2,1)}, f32[128,256]{1,0:T(8,128)}, f32[128,256]{1,0:T(8,128)}) custom-call(bf16[16,64,2048]{2,1,0:T(8,128)(2,1)S(1)} %get-tuple-element.9.refs_0_, f32[128,256]{1,0:T(8,128)S(1)} %get-tuple-element.10.refs_1_, f32[128,256]{1,0:T(8,128)S(1)} %get-tuple-element.11.refs_2_), custom_call_target="tpu_custom_call" | custom-call | tf_op jit(solution)/shard_map/pallas_call | solution.py:426
Async XLA Ops:
  0.6 1.2 %copy-start = (bf16[512,1024]{1,0:T(8,128)(2,1)S(1)}, bf16[512,1024]{1,0:T(8,128)(2,1)}, u32[]{:S(2)}) copy-start(bf16[512,1024]{1,0:T(8,128)(2,1)} %param.3) | copy-start | bytes 3145732
  1.9 0.7 copy-start.1

commit v6 on v5

--- a/solution.py
+++ b/solution.py
@@ -159,7 +159,7 @@
     barrier = pltpu.get_barrier_semaphore()
     for z, yy in row_peers:
         pl.semaphore_signal(barrier, inc=1, device_id=row_device(z, yy), device_id_type=MESH)
-    for xx, z in col_peers:
+    for xx, z in ((ring(x, 1), zh), (ring(x, -1), zh), (x, 1 - zh), (ring(x, 2), zh)):
         pl.semaphore_signal(barrier, inc=1, device_id=col_device(xx, z), device_id_type=MESH)
     across = (lax.rem(r + 8, 16), x * 2 + 1 - zh)
     for device in (sibling, across):
@@ -167,7 +167,7 @@
     read_lists.wait()
     lists[chip] = jnp.zeros((8, 128), jnp.int32)
     lists[chip, :, :K_NB] = own_lists[...]
-    pl.semaphore_wait(barrier, 16)
+    pl.semaphore_wait(barrier, 13)
 
     list_copies, panel_copies = [], []
     for i, (z, yy) in enumerate(row_peers):

time: 99.5 us -> 98.4 us (0.989)
  Pallas kernels: 96.7 us -> 95.6 us
    pallas_call x1, Pallas kernels: 94.6 us -> 93.5 us  [shards(): pl.pallas_call(kernel, out_shape=out_shape, in_specs=[place] * 3, out_spe...]
where the time goes in v6:
time: 98.4 us; the launch traced here: 98.2 us
  Pallas kernels  95.6 us (97%)
  local copies, waits for them, and re-layouts  1.9 us (2%)
    pallas_call x1, Pallas kernels, shards(): pl.pallas_call(kernel, out_shape=out_shape, in_specs=[place] * 3, out_spe...  93.5 us
    pallas_call x1, Pallas kernels, shards(): pl.pallas_call(hand_on, out_shape=out_shape, in_specs=[place] * 3, out_sp...  2.15 us

profile of v6, /device:TPU:1, one launch (start us, length us, event | category | flops | bytes accessed | tf_op | source)
XLA Modules:
  0.0 98.2 jit_solution(11930498979799173689)
XLA Ops:
  0.6 0.0 copy-start
  0.6 1.2 %copy-done = bf16[512,1024]{1,0:T(8,128)(2,1)S(1)} copy-done((bf16[512,1024]{1,0:T(8,128)(2,1)S(1)}, bf16[512,1024]{1,0:T(8,128)(2,1)}, u32[]{:S(2)}) %copy-start) | copy-done | bytes 1048600
  1.9 0.0 copy-start.1
  1.9 0.7 copy-done.1
  2.5 93.5 %shard_map.58 = (bf16[16,64,2048]{2,1,0:T(8,128)(2,1)S(1)}, f32[128,256]{1,0:T(8,128)S(1)}, f32[128,256]{1,0:T(8,128)S(1)}) custom-call(bf16[8,64,1024]{2,1,0:T(8,128)(2,1)S(1)} %bitcast.3, s32[8,26]{1,0:T(8,128)S(1)} %copy-done.1, bf16[16,64,2048]{2,1,0:T(8,128)(2,1)} %bitcast.4), custom_call_target="tpu_custom_call" | custom-call | tf_op jit(solution)/shard_map/pallas_call | solution.py:374
  96.0 2.2 %shard_map.59 = (bf16[16,64,2048]{2,1,0:T(8,128)(2,1)}, f32[128,256]{1,0:T(8,128)}, f32[128,256]{1,0:T(8,128)}) custom-call(bf16[16,64,2048]{2,1,0:T(8,128)(2,1)S(1)} %get-tuple-element.9.refs_0_, f32[128,256]{1,0:T(8,128)S(1)} %get-tuple-element.10.refs_1_, f32[128,256]{1,0:T(8,128)S(1)} %get-tuple-element.11.refs_2_), custom_call_target="tpu_custom_call" | custom-call | tf_op jit(solution)/shard_map/pallas_call | solution.py:426
Async XLA Ops:
  0.6 1.2 %copy-start = (bf16[512,1024]{1,0:T(8,128)(2,1)S(1)}, bf16[512,1024]{1,0:T(8,128)(2,1)}, u32[]{:S(2)}) copy-start(bf16[512,1024]{1,0:T(8,128)(2,1)} %param.3) | copy-start | bytes 3145732
  1.9 0.7 copy-start.1

commit v7 on v6

--- a/solution.py
+++ b/solution.py
@@ -340,11 +340,8 @@
     corr_copies = project(0, fs[pl.ds(c * 16, 16)].reshape(1024, 128))
     gf.need_all()
 
-    @pl.loop(0, 4)
-    def _(j):
-        for i in range(4):
-            column = j * 4 + i
-            image[column] = product(fs, column).astype(jnp.bfloat16)
+    for column in range(16):
+        image[column] = product(fs, column).astype(jnp.bfloat16)
 
     proj_copies = project(1, image[...].reshape(1024, 128))
 

time: 98.4 us -> 98.4 us (level)
  no operation moved by 1% of the time
where the time goes in v7:
time: 98.4 us; the launch traced here: 98.2 us
  Pallas kernels  95.6 us (97%)
  local copies, waits for them, and re-layouts  1.9 us (2%)
    pallas_call x1, Pallas kernels, shards(): pl.pallas_call(kernel, out_shape=out_shape, in_specs=[place] * 3, out_spe...  93.5 us
    pallas_call x1, Pallas kernels, shards(): pl.pallas_call(hand_on, out_shape=out_shape, in_specs=[place] * 3, out_sp...  2.15 us

profile of v7, /device:TPU:1, one launch (start us, length us, event | category | flops | bytes accessed | tf_op | source)
XLA Modules:
  0.0 98.2 jit_solution(8280389486858402076)
XLA Ops:
  0.6 0.0 copy-start
  0.6 1.2 %copy-done = bf16[512,1024]{1,0:T(8,128)(2,1)S(1)} copy-done((bf16[512,1024]{1,0:T(8,128)(2,1)S(1)}, bf16[512,1024]{1,0:T(8,128)(2,1)}, u32[]{:S(2)}) %copy-start) | copy-done | bytes 1048600
  1.9 0.0 copy-start.1
  1.9 0.7 copy-done.1
  2.5 93.5 %shard_map.58 = (bf16[16,64,2048]{2,1,0:T(8,128)(2,1)S(1)}, f32[128,256]{1,0:T(8,128)S(1)}, f32[128,256]{1,0:T(8,128)S(1)}) custom-call(bf16[8,64,1024]{2,1,0:T(8,128)(2,1)S(1)} %bitcast.3, s32[8,26]{1,0:T(8,128)S(1)} %copy-done.1, bf16[16,64,2048]{2,1,0:T(8,128)(2,1)} %bitcast.4), custom_call_target="tpu_custom_call" | custom-call | tf_op jit(solution)/shard_map/pallas_call | solution.py:371
  96.0 2.2 %shard_map.59 = (bf16[16,64,2048]{2,1,0:T(8,128)(2,1)}, f32[128,256]{1,0:T(8,128)}, f32[128,256]{1,0:T(8,128)}) custom-call(bf16[16,64,2048]{2,1,0:T(8,128)(2,1)S(1)} %get-tuple-element.9.refs_0_, f32[128,256]{1,0:T(8,128)S(1)} %get-tuple-element.10.refs_1_, f32[128,256]{1,0:T(8,128)S(1)} %get-tuple-element.11.refs_2_), custom_call_target="tpu_custom_call" | custom-call | tf_op jit(solution)/shard_map/pallas_call | solution.py:423
Async XLA Ops:
  0.6 1.2 %copy-start = (bf16[512,1024]{1,0:T(8,128)(2,1)S(1)}, bf16[512,1024]{1,0:T(8,128)(2,1)}, u32[]{:S(2)}) copy-start(bf16[512,1024]{1,0:T(8,128)(2,1)} %param.3) | copy-start | bytes 3145732
  1.9 0.7 copy-start.1
